TPU v7x, 32 devices: a whole 2x2x4 slice. The times are simulated.
32 devices in a mesh: fsdp: 8 (over y, x, core), tensor: 4 (over z).
Axes of the slice: x: 2, y: 2, z: 4, core: 2. Of those that a mesh axis runs over, the one named last changes fastest.
Arguments:
- tokens: bfloat16 [8192, 1536], P(('fsdp', 'tensor')), may hold values from -6 to 6
- w_query: bfloat16 [1536, 1536], P('fsdp', 'tensor'), may hold values from -0.15625 to 0.15625
- key_weight_matrix: bfloat16 [1536, 768], P('fsdp', 'tensor'), may hold values from -0.15625 to 0.15625
- value_weight_matrix: bfloat16 [1536, 768], P('fsdp', 'tensor'), may hold values from -0.15625 to 0.15625
- w_out: bfloat16 [1536, 1536], P('tensor', 'fsdp'), may hold values from -6 to 6
- w_gate: bfloat16 [1536, 4096], P('fsdp', 'tensor'), may hold values from -0.15625 to 0.15625
- w_up: bfloat16 [1536, 4096], P('fsdp', 'tensor'), may hold values from -0.15625 to 0.15625
- w_down: bfloat16 [4096, 1536], P('tensor', 'fsdp'), may hold values from -0.1875 to 0.1875
- norm_attn: bfloat16 [1536], P('fsdp'), may hold values from 0.5 to 1.5
- norm_ffn: bfloat16 [1536], P('fsdp'), may hold values from 0.5 to 1.5
- grad_out: bfloat16 [8192, 1536], P(('fsdp', 'tensor')), may hold values from -6 to 6
Outputs:
- layer_out: bfloat16 [8192, 1536], P(('fsdp', 'tensor'))
- grad_tokens: bfloat16 [8192, 1536], P(('fsdp', 'tensor'))
- grad_query: float32 [1536, 1536], P('fsdp', 'tensor')
- grad_key: float32 [1536, 768], P('fsdp', 'tensor')
- grad_value: float32 [1536, 768], P('fsdp', 'tensor')
- grad_outproj: float32 [1536, 1536], P('tensor', 'fsdp')
- grad_gate: float32 [1536, 4096], P('fsdp', 'tensor')
- grad_upproj: float32 [1536, 4096], P('fsdp', 'tensor')
- grad_down: float32 [4096, 1536], P('tensor', 'fsdp')
- grad_norm_attn: float32 [1536], P('fsdp')
- grad_norm_ffn: float32 [1536], P('fsdp')
- rms_stats: float32 [3], replicated
All inputs are finite; a program needn't handle non-finite values.
Results may differ from a plain program's by a relative error of at most 0.024.
Values may be sent and summed in bfloat16 or wider, within the bound.
No kernel may reach another device: no remote copies, remote signals or barrier semaphores. Data moves between devices by JAX's collectives and lax.ppermute only.
A program may use at most 192 MiB of HBM per device.

v0:
```python
import jax
import jax.numpy as jnp
from jax import lax
from jax.sharding import PartitionSpec as P

HEAD_WIDTH = 96
SEQUENCE_LENGTH = 4096


EPSILON = 1e-05
ROPE_BASE = 100000.0
MASKED = -1e30


def passed_along(value, axis, steps):
    count = lax.axis_size(axis)
    initial, last = (max(0, -steps), min(count, count - steps))
    return lax.ppermute(value, axis, [(source, source + steps) for source in range(initial, last)])


def rms_norm(values, gain):
    scale_row = lax.rsqrt(jnp.mean(values * values, axis=-1, keepdims=True) + EPSILON)
    return (values * scale_row * gain, scale_row)


def norm_back(values, scale_row, gain, grad_normed):
    weighted = grad_normed * gain
    inner = jnp.mean(weighted * values, axis=-1, keepdims=True)
    grad_values = scale_row * weighted - values * (scale_row * scale_row * scale_row) * inner
    grad_gain = jnp.sum(grad_normed * values * scale_row, axis=0)
    return (grad_values, grad_gain)


def rope_tables(positions, head_size):
    half = head_size // 2
    freq = ROPE_BASE ** (-(jnp.arange(half, dtype=jnp.float32) * 2.0) / head_size)
    angle = positions.astype(jnp.float32)[:, None] * freq[None, :]
    return (jnp.cos(angle)[:, None, :], jnp.sin(angle)[:, None, :])


def rotate(values, cosine, sine):
    half = values.shape[-1] // 2
    first = values[..., :half]
    second = values[..., half:]
    return jnp.concatenate(
        [first * cosine - second * sine, second * cosine + first * sine], axis=-1
    )


def unrotate(grads, cosine, sine):
    half = grads.shape[-1] // 2
    first = grads[..., :half]
    second = grads[..., half:]
    return jnp.concatenate(
        [first * cosine + second * sine, second * cosine - first * sine], axis=-1
    )


def block_scores(query_block, query_pos, keys_all, key_pos, scale):
    scores = (
        jnp.einsum("qgrd,kgd->grqk", query_block, keys_all, preferred_element_type=jnp.float32)
        * scale
    )
    valid = (key_pos[None, :] <= query_pos[:, None]) & (key_pos[None, :] >= 0)
    return jnp.where(valid, scores, MASKED)


def per_device(
    tokens,
    w_query,
    key_weight_matrix,
    value_weight_matrix,
    w_out,
    w_gate,
    w_up,
    w_down,
    norm_attn,
    norm_ffn,
    grad_out,
):
    tensor_count = lax.axis_size("tensor")
    fsdp_count = lax.axis_size("fsdp")
    local_rows = tokens.shape[0]
    width = tokens.shape[1]
    span_rows = local_rows * tensor_count
    group = SEQUENCE_LENGTH // span_rows
    place = lax.axis_index("fsdp") % group
    head_size = HEAD_WIDTH
    query_heads = w_query.shape[1] // head_size
    kv_heads = key_weight_matrix.shape[1] // head_size
    repeat = query_heads // kv_heads
    scale = head_size ** (-0.5)
    block_index = min(512, span_rows)
    blocks = span_rows // block_index
    keys_total = group * span_rows
    gathered = (
        lax.all_gather(w_query, "fsdp", axis=0, tiled=True),
        lax.all_gather(key_weight_matrix, "fsdp", axis=0, tiled=True),
        lax.all_gather(value_weight_matrix, "fsdp", axis=0, tiled=True),
        lax.all_gather(w_out, "fsdp", axis=1, tiled=True),
        lax.all_gather(w_gate, "fsdp", axis=0, tiled=True),
        lax.all_gather(w_up, "fsdp", axis=0, tiled=True),
        lax.all_gather(w_down, "fsdp", axis=1, tiled=True),
        lax.all_gather(norm_attn, "fsdp", axis=0, tiled=True),
        lax.all_gather(norm_ffn, "fsdp", axis=0, tiled=True),
    )
    (
        full_query,
        full_key,
        full_value,
        full_out,
        full_gate,
        full_up,
        full_down,
        gain_first,
        gain_second,
    ) = gathered
    gain_attn = gain_first.astype(jnp.float32)
    gain_ffn = gain_second.astype(jnp.float32)
    resid_in = tokens.astype(jnp.float32)
    first_normed_state, scale_one = rms_norm(resid_in, gain_attn)
    attn_rows = lax.all_gather(
        first_normed_state.astype(jnp.bfloat16), "tensor", axis=0, tiled=True
    )
    query_proj = jnp.dot(attn_rows, full_query, preferred_element_type=jnp.float32)
    key_projected = jnp.dot(attn_rows, full_key, preferred_element_type=jnp.float32)
    value_proj = jnp.dot(attn_rows, full_value, preferred_element_type=jnp.float32)
    positions = place * span_rows + jnp.arange(span_rows, dtype=jnp.int32)
    cosine, sine = rope_tables(positions, head_size)
    query_rotated = rotate(
        query_proj.reshape(span_rows, query_heads, head_size), cosine, sine
    ).astype(jnp.bfloat16)
    key_rotated = rotate(
        key_projected.reshape(span_rows, kv_heads, head_size), cosine, sine
    ).astype(jnp.bfloat16)
    key_flat = key_rotated.reshape(span_rows, kv_heads * head_size)
    value_reduced = value_proj.astype(jnp.bfloat16)
    key_collection = []
    value_list = []
    for offset in range(group - 1, 0, -1):
        moved_key, moved_value = passed_along((key_flat, value_reduced), "fsdp", offset)
        key_collection.append(moved_key)
        value_list.append(moved_value)
    key_collection.append(key_flat)
    value_list.append(value_reduced)
    keys_all = jnp.concatenate(key_collection, axis=0).reshape(keys_total, kv_heads, head_size)
    values_all = jnp.concatenate(value_list, axis=0).reshape(keys_total, kv_heads, head_size)
    key_pos = (place - (group - 1)) * span_rows + jnp.arange(keys_total, dtype=jnp.int32)
    query_block_list = query_rotated.reshape(blocks, block_index, kv_heads, repeat, head_size)
    query_pos = positions.reshape(blocks, block_index)

    def attend(inputs):
        query_block, block_pos = inputs
        scores = block_scores(query_block, block_pos, keys_all, key_pos, scale)
        top = jnp.max(scores, axis=-1, keepdims=True)
        expo = jnp.exp(scores - top)
        denom = jnp.sum(expo, axis=-1, keepdims=True)
        weighted = jnp.einsum(
            "grqk,kgd->qgrd",
            expo.astype(jnp.bfloat16),
            values_all,
            preferred_element_type=jnp.float32,
        )
        return (weighted / jnp.transpose(denom, (2, 0, 1, 3)), top, denom)

    attention_output, tops, denoms = lax.map(attend, (query_block_list, query_pos))
    attended_low = attention_output.reshape(span_rows, query_heads * head_size).astype(jnp.bfloat16)
    attn_part = jnp.dot(attended_low, full_out, preferred_element_type=jnp.float32)
    branch_attn = lax.psum_scatter(
        attn_part.astype(jnp.bfloat16), "tensor", scatter_dimension=0, tiled=True
    ).astype(jnp.float32)
    hidden_state = resid_in + branch_attn
    normed_two, scale_two = rms_norm(hidden_state, gain_ffn)
    ffn_rows = lax.all_gather(normed_two.astype(jnp.bfloat16), "tensor", axis=0, tiled=True)
    gate = jnp.dot(ffn_rows, full_gate, preferred_element_type=jnp.float32)
    up_val = jnp.dot(ffn_rows, full_up, preferred_element_type=jnp.float32)
    sigma = jax.nn.sigmoid(gate)
    swish = gate * sigma
    hidden = (swish * up_val).astype(jnp.bfloat16)
    ffn_part = jnp.dot(hidden, full_down, preferred_element_type=jnp.float32)
    branch_ffn = lax.psum_scatter(
        ffn_part.astype(jnp.bfloat16), "tensor", scatter_dimension=0, tiled=True
    ).astype(jnp.float32)
    result = hidden_state + branch_ffn
    layer_out = result.astype(jnp.bfloat16)
    back_weights = (
        lax.all_gather(w_query, "fsdp", axis=0, tiled=True),
        lax.all_gather(key_weight_matrix, "fsdp", axis=0, tiled=True),
        lax.all_gather(value_weight_matrix, "fsdp", axis=0, tiled=True),
        lax.all_gather(w_out, "fsdp", axis=1, tiled=True),
        lax.all_gather(w_gate, "fsdp", axis=0, tiled=True),
        lax.all_gather(w_up, "fsdp", axis=0, tiled=True),
        lax.all_gather(w_down, "fsdp", axis=1, tiled=True),
        lax.all_gather(norm_attn, "fsdp", axis=0, tiled=True),
        lax.all_gather(norm_ffn, "fsdp", axis=0, tiled=True),
    )
    (
        back_query,
        back_key,
        back_value,
        back_out,
        back_gate,
        back_up,
        back_down,
        back_gain_one,
        back_gain_two,
    ) = back_weights
    grad_rows_ffn = lax.all_gather(grad_out, "tensor", axis=0, tiled=True)
    grad_hidden = jnp.dot(grad_rows_ffn, back_down.T, preferred_element_type=jnp.float32)
    grad_down_w = jnp.dot(hidden.T, grad_rows_ffn, preferred_element_type=jnp.float32)
    grad_gate_pre = (grad_hidden * up_val * (sigma * (1.0 + gate * (1.0 - sigma)))).astype(
        jnp.bfloat16
    )
    grad_up_pre = (grad_hidden * swish).astype(jnp.bfloat16)
    grad_gate_w = jnp.dot(ffn_rows.T, grad_gate_pre, preferred_element_type=jnp.float32)
    grad_up_w = jnp.dot(ffn_rows.T, grad_up_pre, preferred_element_type=jnp.float32)
    grad_two_rows = jnp.dot(
        grad_gate_pre, back_gate.T, preferred_element_type=jnp.float32
    ) + jnp.dot(grad_up_pre, back_up.T, preferred_element_type=jnp.float32)
    grad_normed_two = lax.psum_scatter(
        grad_two_rows.astype(jnp.bfloat16), "tensor", scatter_dimension=0, tiled=True
    ).astype(jnp.float32)
    grad_state_norm, grad_gain_two = norm_back(
        hidden_state, scale_two, back_gain_two.astype(jnp.float32), grad_normed_two
    )
    grad_state = grad_out.astype(jnp.float32) + grad_state_norm
    grad_rows_attn = lax.all_gather(grad_state.astype(jnp.bfloat16), "tensor", axis=0, tiled=True)
    grad_attended = jnp.dot(grad_rows_attn, back_out.T, preferred_element_type=jnp.float32)
    grad_out_w = jnp.dot(attended_low.T, grad_rows_attn, preferred_element_type=jnp.float32)
    grad_attended_blocks = grad_attended.reshape(blocks, block_index, kv_heads, repeat, head_size)

    def attend_back(carry, inputs):
        grad_keys, grad_values = carry
        query_block, block_pos, kept_result, top, denom, grad_result = inputs
        scores = block_scores(query_block, block_pos, keys_all, key_pos, scale)
        expo = jnp.exp(scores - top)
        denom_rows = jnp.transpose(denom, (2, 0, 1, 3))
        grad_weighted = (grad_result / denom_rows).astype(jnp.bfloat16)
        delta = jnp.sum(grad_result * kept_result, axis=-1, keepdims=True) / denom_rows
        delta = jnp.transpose(delta, (1, 2, 0, 3))
        through = jnp.einsum(
            "qgrd,kgd->grqk", grad_weighted, values_all, preferred_element_type=jnp.float32
        )
        grad_scores = (expo * (through - delta)).astype(jnp.bfloat16)
        grad_query_block = (
            jnp.einsum("grqk,kgd->qgrd", grad_scores, keys_all, preferred_element_type=jnp.float32)
            * scale
        )
        grad_keys = (
            grad_keys
            + jnp.einsum(
                "grqk,qgrd->kgd", grad_scores, query_block, preferred_element_type=jnp.float32
            )
            * scale
        )
        grad_values = grad_values + jnp.einsum(
            "grqk,qgrd->kgd",
            expo.astype(jnp.bfloat16),
            grad_weighted,
            preferred_element_type=jnp.float32,
        )
        return ((grad_keys, grad_values), grad_query_block)

    zero_keys = jnp.zeros((keys_total, kv_heads, head_size), jnp.float32)
    (grad_keys_all, grad_values_all), grad_query_rot = lax.scan(
        attend_back,
        (zero_keys, zero_keys),
        (query_block_list, query_pos, attention_output, tops, denoms, grad_attended_blocks),
    )
    grad_key_spans = grad_keys_all.reshape(group, span_rows, kv_heads * head_size)
    grad_value_spans = grad_values_all.reshape(group, span_rows, kv_heads * head_size)
    own_key = grad_key_spans[group - 1]
    own_value = grad_value_spans[group - 1]
    for offset in range(1, group):
        back_key_part, back_value_part = (
            passed_along(
                grad_key_spans[group - 1 - offset].astype(jnp.bfloat16), "fsdp", -offset
            ).astype(jnp.float32),
            passed_along(
                grad_value_spans[group - 1 - offset].astype(jnp.bfloat16), "fsdp", -offset
            ).astype(jnp.float32),
        )
        own_key = own_key + back_key_part
        own_value = own_value + back_value_part
    grad_qproj = unrotate(grad_query_rot.reshape(span_rows, query_heads, head_size), cosine, sine)
    grad_qproj = grad_qproj.reshape(span_rows, query_heads * head_size).astype(jnp.bfloat16)
    grad_kproj = unrotate(own_key.reshape(span_rows, kv_heads, head_size), cosine, sine)
    grad_kproj = grad_kproj.reshape(span_rows, kv_heads * head_size).astype(jnp.bfloat16)
    grad_vproj = own_value.astype(jnp.bfloat16)
    grad_query_w = jnp.dot(attn_rows.T, grad_qproj, preferred_element_type=jnp.float32)
    grad_key_w = jnp.dot(attn_rows.T, grad_kproj, preferred_element_type=jnp.float32)
    grad_value_w = jnp.dot(attn_rows.T, grad_vproj, preferred_element_type=jnp.float32)
    grad_one_rows = (
        jnp.dot(grad_qproj, back_query.T, preferred_element_type=jnp.float32)
        + jnp.dot(grad_kproj, back_key.T, preferred_element_type=jnp.float32)
        + jnp.dot(grad_vproj, back_value.T, preferred_element_type=jnp.float32)
    )
    grad_normed_one = lax.psum_scatter(
        grad_one_rows.astype(jnp.bfloat16), "tensor", scatter_dimension=0, tiled=True
    ).astype(jnp.float32)
    grad_resid, grad_gain_one = norm_back(
        resid_in, scale_one, back_gain_one.astype(jnp.float32), grad_normed_one
    )
    grad_tokens = (grad_state + grad_resid).astype(jnp.bfloat16)
    shards = (
        lax.psum_scatter(
            grad_query_w.astype(jnp.bfloat16), "fsdp", scatter_dimension=0, tiled=True
        ).astype(jnp.float32),
        lax.psum_scatter(
            grad_key_w.astype(jnp.bfloat16), "fsdp", scatter_dimension=0, tiled=True
        ).astype(jnp.float32),
        lax.psum_scatter(
            grad_value_w.astype(jnp.bfloat16), "fsdp", scatter_dimension=0, tiled=True
        ).astype(jnp.float32),
        lax.psum_scatter(
            grad_out_w.astype(jnp.bfloat16), "fsdp", scatter_dimension=1, tiled=True
        ).astype(jnp.float32),
        lax.psum_scatter(
            grad_gate_w.astype(jnp.bfloat16), "fsdp", scatter_dimension=0, tiled=True
        ).astype(jnp.float32),
        lax.psum_scatter(
            grad_up_w.astype(jnp.bfloat16), "fsdp", scatter_dimension=0, tiled=True
        ).astype(jnp.float32),
        lax.psum_scatter(
            grad_down_w.astype(jnp.bfloat16), "fsdp", scatter_dimension=1, tiled=True
        ).astype(jnp.float32),
    )
    squares = jnp.stack(
        [
            jnp.sum(result * result),
            jnp.sum(branch_attn * branch_attn),
            jnp.sum(branch_ffn * branch_ffn),
        ]
    )
    summed_one, summed_two, summed_squares = lax.psum(
        (grad_gain_one, grad_gain_two, squares), ("fsdp", "tensor")
    )
    shard_len = norm_attn.shape[0]
    shard_start = lax.axis_index("fsdp") * shard_len
    gain_grad_one = lax.dynamic_slice_in_dim(summed_one, shard_start, shard_len)
    gain_grad_two = lax.dynamic_slice_in_dim(summed_two, shard_start, shard_len)
    entries = local_rows * width * fsdp_count * tensor_count
    rms_stats = jnp.sqrt(summed_squares / entries)
    return (
        layer_out,
        grad_tokens,
        shards[0],
        shards[1],
        shards[2],
        shards[3],
        shards[4],
        shards[5],
        shards[6],
        gain_grad_one,
        gain_grad_two,
        rms_stats,
    )


def solution(mesh):
    return jax.shard_map(
        per_device,
        mesh=mesh,
        in_specs=(
            P(("fsdp", "tensor"), None),
            P("fsdp", "tensor"),
            P("fsdp", "tensor"),
            P("fsdp", "tensor"),
            P("tensor", "fsdp"),
            P("fsdp", "tensor"),
            P("fsdp", "tensor"),
            P("tensor", "fsdp"),
            P("fsdp"),
            P("fsdp"),
            P(("fsdp", "tensor"), None),
        ),
        out_specs=(
            P(("fsdp", "tensor"), None),
            P(("fsdp", "tensor"), None),
            P("fsdp", "tensor"),
            P("fsdp", "tensor"),
            P("fsdp", "tensor"),
            P("tensor", "fsdp"),
            P("fsdp", "tensor"),
            P("fsdp", "tensor"),
            P("tensor", "fsdp"),
            P("fsdp"),
            P("fsdp"),
            P(),
        ),
        check_vma=False,
    )
```

profile of v0, /device:TPU:0, one launch (start us, length us, event | category | flops | bytes accessed | tf_op | source)
XLA Modules:
  0.0 1282.1 jit_solution(2061009321682606751)
XLA Ops:
  12.9 16.0 %all-reduce.3 = (bf16[1536]{0:T(1024)(128)(2,1)S(1)}, bf16[1536]{0:T(1024)(128)(2,1)}) all-reduce(bf16[1536]{0:T(1024)(128)(2,1)S(1)} %dynamic-update-slice, bf16[1536]{0:T(1024)(128)(2,1)S(1)} %dynamic-update-slice.1), channel_id=1, replica_groups=mesh['fsdp'=8,'tensor'=4] {'fsdp'}, use_global_device_ids=true, to_apply=%add | all-reduce | flops 3072 | bytes 12288
  56.5 38.3 %all-gather.10.cloned.1.call-done = bf16[1024,1536]{1,0:T(8,128)(2,1)} async-done(((bf16[256,1536]{1,0:T(8,128)(2,1)}), bf16[1024,1536]{1,0:T(8,128)(2,1)}) %all-gather.10.cloned.1.call-update) | async-done | bytes 3145744 | tf_op jit(solution)/shard_map/all_gather | solution.py:122
  115.7 24.1 %all-gather.12.cloned.1.call-done = bf16[1536,384]{1,0:T(8,128)(2,1)} async-done(((bf16[192,384]{1,0:T(8,128)(2,1)}), bf16[1536,384]{1,0:T(8,128)(2,1)}) %all-gather.12.cloned.1.call-update) | async-done | bytes 1179664 | tf_op jit(solution)/shard_map/all_gather | solution.py:97
  156.4 96.1 %while.30 = (s32[]{:T(128)}, f32[2,512,2,2,96]{1,4,3,2,0:T(8,128)}, f32[2,2,2,512,1]{3,2,1,4,0:T(2,128)S(1)}, f32[2,2,2,512,1]{3,2,1,4,0:T(2,128)S(1)}, s32[2,51...) while((s32[]{:T(128)}, f32[2,512,2,2,96]{1,4,3,2,0:T(8,128)}, ...), condition=%wide.region_4.5_spmd.clone, body=%wide.region_1.4_spmd.clone.sunk | while | flops 3317899264 | bytes 113498232 | solution.py:166
  158.0 15.2 %bitcast_reduce_fusion.2 = (f32[2,2,512]{2,1,0:T(2,128)S(1)}, f32[2,512,2,4096]{3,1,2,0:T(8,128)}) fusion(pred[512,4096]{1,0:T(8,128)(4,1)S(1)} %compare_and_fusion.4, bf16[4096,2,96]{0,2,1:T(8,128)(2,1)} %get-tuple-element.495, bf16[2,512,2,2,96]{1,4,3,2,0:T(8,128)(2,1)} %get-tuple-element.494, s32[]{:T(128)S(6)} %copy.75), kind=kOutput, calls=%fused_computation.3.clone.1 | convolution fusion | flops 1635776512 | bytes 37625860 | tf_op jit(solution)/shard_map/while/body/eval_jaxpr/qgrd,kgd->grqk/dot_general | solution.py:61
  173.2 15.1 %fusion.178 = f32[2,2,512]{2,1,0:T(2,128)S(1)} fusion(f32[2,512,2,4096]{3,1,2,0:T(8,128)} %get-tuple-element.450, f32[2,2,512]{2,1,0:T(2,128)S(1)} %get-tuple-element.451, pred[512,4096]{1,0:T(8,128)(4,1)S(1)} %compare_and_fusion.4), kind=kLoop, calls=%fused_computation.6.clone.1 | loop fusion | flops 33552384 | bytes 35667968 | tf_op jit(solution)/shard_map/while/body/eval_jaxpr/reduce_sum | solution.py:157
  188.3 16.0 %fusion.179 = f32[2,512,2,2,96]{1,4,3,2,0:T(8,128)} fusion(f32[2,512,2,2,96]{1,4,3,2,0:T(8,128)} %get-tuple-element.480, s32[]{:T(128)S(6)} %copy.75, bf16[4096,2,96]{0,2,1:T(8,128)(2,1)} %get-tuple-element.496, f32[2,512,2,4096]{3,1,2,0:T(8,128)} %get-tuple-element.450, f32[2,2,512]{2,1,0:T(2,128)S(1)} %get-tuple-element.451, ...), kind=kOutput, calls=%fused_computation.17.clone.1 | convolution fusion | flops 1644363776 | bytes 38027268 | tf_op jit(solution)/shard_map/while/body/eval_jaxpr/grqk,kgd->qgrd/dot_general | solution.py:158
  205.8 15.2 %bitcast_reduce_fusion.2 = (f32[2,2,512]{2,1,0:T(2,128)S(1)}, f32[2,512,2,4096]{3,1,2,0:T(8,128)}) fusion(pred[512,4096]{1,0:T(8,128)(4,1)S(1)} %compare_and_fusion.4, bf16[4096,2,96]{0,2,1:T(8,128)(2,1)} %get-tuple-element.495, bf16[2,512,2,2,96]{1,4,3,2,0:T(8,128)(2,1)} %get-tuple-element.494, s32[]{:T(128)S(6)} %copy.75), kind=kOutput, calls=%fused_computation.3.clone.1 | convolution fusion | flops 1635776512 | bytes 37625860 | tf_op jit(solution)/shard_map/while/body/eval_jaxpr/qgrd,kgd->grqk/dot_general | solution.py:61
  221.0 15.1 %fusion.178 = f32[2,2,512]{2,1,0:T(2,128)S(1)} fusion(f32[2,512,2,4096]{3,1,2,0:T(8,128)} %get-tuple-element.450, f32[2,2,512]{2,1,0:T(2,128)S(1)} %get-tuple-element.451, pred[512,4096]{1,0:T(8,128)(4,1)S(1)} %compare_and_fusion.4), kind=kLoop, calls=%fused_computation.6.clone.1 | loop fusion | flops 33552384 | bytes 35667968 | tf_op jit(solution)/shard_map/while/body/eval_jaxpr/reduce_sum | solution.py:157
  236.1 16.0 %fusion.179 = f32[2,512,2,2,96]{1,4,3,2,0:T(8,128)} fusion(f32[2,512,2,2,96]{1,4,3,2,0:T(8,128)} %get-tuple-element.480, s32[]{:T(128)S(6)} %copy.75, bf16[4096,2,96]{0,2,1:T(8,128)(2,1)} %get-tuple-element.496, f32[2,512,2,4096]{3,1,2,0:T(8,128)} %get-tuple-element.450, f32[2,2,512]{2,1,0:T(2,128)S(1)} %get-tuple-element.451, ...), kind=kOutput, calls=%fused_computation.17.clone.1 | convolution fusion | flops 1644363776 | bytes 38027268 | tf_op jit(solution)/shard_map/while/body/eval_jaxpr/grqk,kgd->qgrd/dot_general | solution.py:158
  261.3 66.5 %reduce-scatter.12.cloned.1.call-done = bf16[256,1536]{1,0:T(8,128)(2,1)} async-done(((bf16[1024,1536]{1,0:T(8,128)(2,1)}), bf16[256,1536]{1,0:T(8,128)(2,1)}) %reduce-scatter.12.cloned.1.call-update) | async-done | bytes 786448 | tf_op jit(solution)/shard_map/reduce_scatter | solution.py:169
  333.9 28.0 %all-gather.20.cloned.1.call-done = bf16[1536,1024]{1,0:T(8,128)(2,1)} async-done(((bf16[192,1024]{1,0:T(8,128)(2,1)}), bf16[1536,1024]{1,0:T(8,128)(2,1)}) %all-gather.20.cloned.1.call-update) | async-done | bytes 3145744 | tf_op jit(solution)/shard_map/all_gather | solution.py:102
  362.0 65.5 %all-gather.16.cloned.1.call-done = bf16[1024,1536]{1,0:T(8,128)(2,1)} async-done(((bf16[256,1536]{1,0:T(8,128)(2,1)}), bf16[1024,1536]{1,0:T(8,128)(2,1)}) %all-gather.16.cloned.1.call-update) | async-done | bytes 3145744 | tf_op jit(solution)/shard_map/all_gather | solution.py:174
  435.8 24.6 %all-gather.18.cloned.1.call-done = bf16[1536,1024]{1,0:T(8,128)(2,1)} async-done(((bf16[192,1024]{1,0:T(8,128)(2,1)}), bf16[1536,1024]{1,0:T(8,128)(2,1)}) %all-gather.18.cloned.1.call-update) | async-done | bytes 3145744 | tf_op jit(solution)/shard_map/all_gather | solution.py:101
  468.6 56.9 %all-gather.24.cloned.1.call-done = bf16[1024,1536]{1,0:T(8,128)(2,1)} async-done(((bf16[256,1536]{1,0:T(8,128)(2,1)}), bf16[1024,1536]{1,0:T(8,128)(2,1)}) %all-gather.24.cloned.1.call-update) | async-done | bytes 3145744 | tf_op jit(solution)/shard_map/all_gather | solution.py:208
  525.5 32.9 %all-gather.22.cloned.1.call-done = bf16[1024,1536]{0,1:T(8,128)(2,1)} async-done(((bf16[1024,192]{0,1:T(8,128)(2,1)}), bf16[1024,1536]{0,1:T(8,128)(2,1)}) %all-gather.22.cloned.1.call-update) | async-done | bytes 3145744 | tf_op jit(solution)/shard_map/all_gather | solution.py:103
  588.2 49.2 %reduce-scatter.14.cloned.1.call-done = bf16[256,1536]{1,0:T(8,128)(2,1)} async-done(((bf16[1024,1536]{1,0:T(8,128)(2,1)}), bf16[256,1536]{1,0:T(8,128)(2,1)}) %reduce-scatter.14.cloned.1.call-update) | async-done | bytes 786448 | tf_op jit(solution)/shard_map/reduce_scatter | solution.py:181
  637.4 62.6 %reduce-scatter.16.cloned.1.call-done = bf16[256,1536]{1,0:T(8,128)(2,1)} async-done(((bf16[1024,1536]{1,0:T(8,128)(2,1)}), bf16[256,1536]{1,0:T(8,128)(2,1)}) %reduce-scatter.16.cloned.1.call-update) | async-done | bytes 786448 | tf_op jit(solution)/shard_map/reduce_scatter | solution.py:220
  728.6 40.8 %all-gather.26.cloned.1.call-done = bf16[1024,1536]{1,0:T(8,128)(2,1)} async-done(((bf16[256,1536]{1,0:T(8,128)(2,1)}), bf16[1024,1536]{1,0:T(8,128)(2,1)}) %all-gather.26.cloned.1.call-update) | async-done | bytes 3145744 | tf_op jit(solution)/shard_map/all_gather | solution.py:227
  777.4 189.5 %while.31 = (s32[]{:T(128)}, f32[4096,2,96]{0,2,1:T(8,128)}, f32[4096,2,96]{0,2,1:T(8,128)}, f32[2,512,2,2,96]{1,0,4,3,2:T(2,128)}, bf16[2,512,2,2,96]{1,4,3,2,0...) while((s32[]{:T(128)}, f32[4096,2,96]{0,2,1:T(8,128)}, ...), condition=%wide.region_12.13_spmd.clone, body=%wide.region_10.12_spmd.clone.sunk | while | flops 8146464768 | bytes 251287760 | solution.py:265
  799.0 17.9 %fusion.193 = f32[4096,2,96]{0,2,1:T(8,128)} fusion(f32[2,512,2,4096]{3,1,2,0:T(8,128)} %fusion.188, f32[2,2,512]{2,1,0:T(2,128)S(1)} %get-tuple-element.467, pred[512,4096]{1,0:T(8,128)(4,1)} %compare_and_fusion.5, f32[4096,2,96]{0,2,1:T(8,128)} %get-tuple-element.516, pred[]{:T(512)S(6)} %compare.4, ...), kind=kOutput, calls=%fused_computation.42.clone.1 | convolution fusion | flops 1646133248 | bytes 42745856 | tf_op jit(solution)/shard_map/while/body/eval_jaxpr/grqk,qgrd->kgd/dot_general | solution.py:256
  817.0 22.0 %fusion.191 = bf16[2,2,512,4096]{3,2,1,0:T(8,128)(2,1)} fusion(f32[2,512,2,4096]{3,1,2,0:T(8,128)} %fusion.188, f32[2,2,512]{2,1,0:T(2,128)S(1)} %fusion.190, f32[2,2,512]{2,1,0:T(2,128)S(1)} %get-tuple-element.467, pred[512,4096]{1,0:T(8,128)(4,1)} %compare_and_fusion.5, bf16[4096,2,96]{0,2,1:T(8,128)(2,1)} %get-tuple-element.539, ...), kind=kOutput, calls=%fused_computation.30.clone.1 | convolution fusion | flops 1661337600 | bytes 54812672 | tf_op jit(solution)/shard_map/while/body/eval_jaxpr/qgrd,kgd->grqk/dot_general | solution.py:241
  856.6 15.0 %dynamic_update_slice.26 = f32[2,512,2,2,96]{1,0,4,3,2:T(2,128)} dynamic-update-slice(f32[2,512,2,2,96]{1,0,4,3,2:T(2,128)} %get-tuple-element.517, f32[1,512,2,2,96]{1,0,4,3,2:T(1,128)S(1)} %copy.64, s32[]{:T(128)S(6)} %copy.87, s32[]{:T(128)} %constant.84.clone.1..sunk, s32[]{:T(128)} %constant.84.clone.1..sunk, s32[]{:T(128)} %constant.84.clone.1..sunk, s32[]{:T(128)} %constant.84.clone.1..sunk) | dynamic-update-slice | bytes 1572868 | tf_op jit(solution)/shard_map/while/body/jit(dynamic_update_index_in_dim)/dynamic_update_slice | solution.py:166
  878.0 15.0 %fusion.188 = f32[2,512,2,4096]{3,1,2,0:T(8,128)} fusion(bf16[4096,2,96]{0,2,1:T(8,128)(2,1)S(1)} %get-tuple-element.535, bf16[2,512,2,2,96]{1,4,3,2,0:T(8,128)(2,1)} %get-tuple-element.533, s32[]{:T(128)S(6)} %copy.87), kind=kOutput, calls=%fused_computation.46.clone.1 | convolution fusion | flops 1610612736 | bytes 35520516 | tf_op jit(solution)/shard_map/while/body/eval_jaxpr/qgrd,kgd->grqk/dot_general | solution.py:61
  893.0 18.9 %fusion.193 = f32[4096,2,96]{0,2,1:T(8,128)} fusion(f32[2,512,2,4096]{3,1,2,0:T(8,128)} %fusion.188, f32[2,2,512]{2,1,0:T(2,128)S(1)} %get-tuple-element.467, pred[512,4096]{1,0:T(8,128)(4,1)} %compare_and_fusion.5, f32[4096,2,96]{0,2,1:T(8,128)} %get-tuple-element.516, pred[]{:T(512)S(6)} %compare.4, ...), kind=kOutput, calls=%fused_computation.42.clone.1 | convolution fusion | flops 1646133248 | bytes 42745856 | tf_op jit(solution)/shard_map/while/body/eval_jaxpr/grqk,qgrd->kgd/dot_general | solution.py:256
  911.9 21.6 %fusion.191 = bf16[2,2,512,4096]{3,2,1,0:T(8,128)(2,1)} fusion(f32[2,512,2,4096]{3,1,2,0:T(8,128)} %fusion.188, f32[2,2,512]{2,1,0:T(2,128)S(1)} %fusion.190, f32[2,2,512]{2,1,0:T(2,128)S(1)} %get-tuple-element.467, pred[512,4096]{1,0:T(8,128)(4,1)} %compare_and_fusion.5, bf16[4096,2,96]{0,2,1:T(8,128)(2,1)} %get-tuple-element.539, ...), kind=kOutput, calls=%fused_computation.30.clone.1 | convolution fusion | flops 1661337600 | bytes 54812672 | tf_op jit(solution)/shard_map/while/body/eval_jaxpr/qgrd,kgd->grqk/dot_general | solution.py:241
  951.9 14.9 %dynamic_update_slice.26 = f32[2,512,2,2,96]{1,0,4,3,2:T(2,128)} dynamic-update-slice(f32[2,512,2,2,96]{1,0,4,3,2:T(2,128)} %get-tuple-element.517, f32[1,512,2,2,96]{1,0,4,3,2:T(1,128)S(1)} %copy.64, s32[]{:T(128)S(6)} %copy.87, s32[]{:T(128)} %constant.84.clone.1..sunk, s32[]{:T(128)} %constant.84.clone.1..sunk, s32[]{:T(128)} %constant.84.clone.1..sunk, s32[]{:T(128)} %constant.84.clone.1..sunk) | dynamic-update-slice | bytes 1572868 | tf_op jit(solution)/shard_map/while/body/jit(dynamic_update_index_in_dim)/dynamic_update_slice | solution.py:166
  1048.4 36.7 %reduce-scatter.24.cloned.1.call-done = bf16[192,192]{1,0:T(8,128)(2,1)} async-done(((bf16[1536,192]{1,0:T(8,128)(2,1)}), bf16[192,192]{1,0:T(8,128)(2,1)}) %reduce-scatter.24.cloned.1.call-update) | async-done | bytes 73744 | tf_op jit(solution)/shard_map/reduce_scatter | solution.py:312
  1086.7 38.6 %reduce-scatter.26.cloned.1.call-done = bf16[384,192]{0,1:T(8,128)(2,1)} async-done(((bf16[384,1536]{0,1:T(8,128)(2,1)}), bf16[384,192]{0,1:T(8,128)(2,1)}) %reduce-scatter.26.cloned.1.call-update) | async-done | bytes 147472 | tf_op jit(solution)/shard_map/reduce_scatter | solution.py:315
  1127.0 38.4 %reduce-scatter.20.cloned.1.call-done = bf16[192,384]{1,0:T(8,128)(2,1)} async-done(((bf16[1536,384]{1,0:T(8,128)(2,1)}), bf16[192,384]{1,0:T(8,128)(2,1)}) %reduce-scatter.20.cloned.1.call-update) | async-done | bytes 147472 | tf_op jit(solution)/shard_map/reduce_scatter | solution.py:306
  1167.0 60.9 %reduce-scatter.18.cloned.1.call-done = bf16[256,1536]{1,0:T(8,128)(2,1)} async-done(((bf16[1024,1536]{1,0:T(8,128)(2,1)}), bf16[256,1536]{1,0:T(8,128)(2,1)}) %reduce-scatter.18.cloned.1.call-update) | async-done | bytes 786448 | tf_op jit(solution)/shard_map/reduce_scatter | solution.py:298
  1229.5 40.6 %all-reduce.2 = (f32[1536]{0:T(1024)S(1)}, f32[1536]{0:T(1024)S(1)}, f32[3]{0:T(128)S(1)}) all-reduce(f32[1536]{0:T(1024)S(1)} %get-tuple-element.240, f32[1536]{0:T(1024)S(1)} %copy-done.34, f32[3]{0:T(128)S(1)} %pad_maximum_fusion.5), channel_id=1, replica_groups=mesh['fsdp'=8,'tensor'=4] {'fsdp','tensor'}, use_global_device_ids=true, to_apply=%region_23.24 | all-reduce | flops 3075 | bytes 24600 | tf_op jit(solution)/shard_map/psum | solution.py:335
  (295 shorter events, 326.5 us)
Async XLA Ops:
  7.2 87.6 %all-gather.10.cloned.1.call-start = ((), (), s32[]{:S(2)}) async-start(), calls=%async_computation.11 | async-start | bytes 3932160 | tf_op jit(solution)/shard_map/all_gather | solution.py:122
  31.8 108.1 %all-gather.12.cloned.1.call-start = ((), (), s32[]{:S(2)}) async-start(), calls=%async_computation.12 | async-start | bytes 1327104 | tf_op jit(solution)/shard_map/all_gather | solution.py:97
  32.5 222.5 %all-gather.14.cloned.1.call-start = ((), (), s32[]{:S(2)}) async-start(), calls=%async_computation.13 | async-start | bytes 1327104 | tf_op jit(solution)/shard_map/all_gather | solution.py:100
  33.2 294.6 %reduce-scatter.12.cloned.1.call-start = ((), (), s32[]{:S(2)}) async-start(), calls=%async_computation.14 | async-start | bytes 3932160 | tf_op jit(solution)/shard_map/reduce_scatter | solution.py:169
  98.9 50.6 %collective-permute-start.5 = (bf16[1024,192]{0,1:T(8,128)(2,1)}, bf16[1024,192]{0,1:T(8,128)(2,1)}, u32[]{:S(2)}, u32[]{:S(2)}) collective-permute-start(bf16[1024,192]{0,1:T(8,128)(2,1)} %convolution_convert_fusion.9), channel_id=1, source_target_pairs={{0,4},{4,8},{8,12},{12,16},{16,20},{20,24},{24,28},{1,5},{5,9},{9,... | collective-permute-start | bytes 1179656 | tf_op jit(solution)/shard_map/ppermute | solution.py:18
  101.4 48.2 %collective-permute-start.4 = (bf16[1024,192]{0,1:T(8,128)(2,1)}, bf16[1024,192]{0,1:T(8,128)(2,1)}, u32[]{:S(2)}, u32[]{:S(2)}) collective-permute-start(bf16[1024,192]{0,1:T(8,128)(2,1)} %convolution_convert_fusion.9), channel_id=1, source_target_pairs={{0,8},{4,12},{8,16},{12,20},{16,24},{20,28},{1,9},{5,13},{9,17},{1... | collective-permute-start | bytes 1179656 | tf_op jit(solution)/shard_map/ppermute | solution.py:18
  107.1 38.3 %collective-permute-start.2 = (bf16[1024,192]{0,1:T(8,128)(2,1)}, bf16[1024,192]{0,1:T(8,128)(2,1)}, u32[]{:S(2)}, u32[]{:S(2)}) collective-permute-start(bf16[1024,192]{0,1:T(8,128)(2,1)} %bitcast.3), channel_id=1, source_target_pairs={{0,4},{4,8},{8,12},{12,16},{16,20},{20,24},{24,28},{1,5},{5,9},{9,... | collective-permute-start | bytes 1179656 | tf_op jit(solution)/shard_map/ppermute | solution.py:18
  111.1 35.8 %collective-permute-start.1 = (bf16[1024,192]{0,1:T(8,128)(2,1)}, bf16[1024,192]{0,1:T(8,128)(2,1)}, u32[]{:S(2)}, u32[]{:S(2)}) collective-permute-start(bf16[1024,192]{0,1:T(8,128)(2,1)} %bitcast.3), channel_id=1, source_target_pairs={{0,8},{4,12},{8,16},{12,20},{16,24},{20,28},{1,9},{5,13},{9,17},{1... | collective-permute-start | bytes 1179656 | tf_op jit(solution)/shard_map/ppermute | solution.py:18
  113.7 33.2 %collective-permute-start = (bf16[1024,192]{0,1:T(8,128)(2,1)}, bf16[1024,192]{0,1:T(8,128)(2,1)}, u32[]{:S(2)}, u32[]{:S(2)}) collective-permute-start(bf16[1024,192]{0,1:T(8,128)(2,1)} %bitcast.3), channel_id=1, source_target_pairs={{0,12},{4,16},{8,20},{12,24},{16,28},{1,13},{5,17},{9,21},{13,25},... | collective-permute-start | bytes 1179656 | tf_op jit(solution)/shard_map/ppermute | solution.py:18
  145.4 8.5 collective-permute-start.3
  260.7 101.3 %all-gather.20.cloned.1.call-start = ((), (), s32[]{:S(2)}) async-start(), calls=%async_computation.17 | async-start | bytes 3538944 | tf_op jit(solution)/shard_map/all_gather | solution.py:102
  261.3 166.2 %all-gather.16.cloned.1.call-start = ((), (), s32[]{:S(2)}) async-start(), calls=%async_computation.15 | async-start | bytes 3932160 | tf_op jit(solution)/shard_map/all_gather | solution.py:174
  331.7 128.7 %all-gather.18.cloned.1.call-start = ((), (), s32[]{:S(2)}) async-start(), calls=%async_computation.16 | async-start | bytes 3538944 | tf_op jit(solution)/shard_map/all_gather | solution.py:101
  332.4 193.1 %all-gather.24.cloned.1.call-start = ((), (), s32[]{:S(2)}) async-start(), calls=%async_computation.20 | async-start | bytes 3932160 | tf_op jit(solution)/shard_map/all_gather | solution.py:208
  333.2 225.2 %all-gather.22.cloned.1.call-start = ((), (), s32[]{:S(2)}) async-start(), calls=%async_computation.18 | async-start | bytes 3538944 | tf_op jit(solution)/shard_map/all_gather | solution.py:103
  333.9 303.5 %reduce-scatter.14.cloned.1.call-start = ((), (), s32[]{:S(2)}) async-start(), calls=%async_computation.19 | async-start | bytes 3932160 | tf_op jit(solution)/shard_map/reduce_scatter | solution.py:181
  577.0 123.0 %reduce-scatter.16.cloned.1.call-start = ((), (), s32[]{:S(2)}) async-start(), calls=%async_computation.21 | async-start | bytes 3932160 | tf_op jit(solution)/shard_map/reduce_scatter | solution.py:220
  588.2 181.2 %all-gather.26.cloned.1.call-start = ((), (), s32[]{:S(2)}) async-start(), calls=%async_computation.22 | async-start | bytes 3932160 | tf_op jit(solution)/shard_map/all_gather | solution.py:227
  705.7 324.4 %reduce-scatter.32.cloned.1.call-start = ((), (), s32[]{:S(2)}) async-start(), calls=%async_computation.30 | async-start | bytes 3538944 | tf_op jit(solution)/shard_map/reduce_scatter | solution.py:324
  713.4 318.8 %reduce-scatter.30.cloned.1.call-start = ((), (), s32[]{:S(2)}) async-start(), calls=%async_computation.29 | async-start | bytes 3538944 | tf_op jit(solution)/shard_map/reduce_scatter | solution.py:321
  721.9 312.2 %reduce-scatter.28.cloned.1.call-start = ((), (), s32[]{:S(2)}) async-start(), calls=%async_computation.28 | async-start | bytes 3538944 | tf_op jit(solution)/shard_map/reduce_scatter | solution.py:318
  728.6 318.2 %reduce-scatter.22.cloned.1.call-start = ((), (), s32[]{:S(2)}) async-start(), calls=%async_computation.25 | async-start | bytes 884736 | tf_op jit(solution)/shard_map/reduce_scatter | solution.py:309
  969.2 12.1 collective-permute-start.8
  970.7 11.8 collective-permute-start.6
  972.0 20.6 %collective-permute-start.7 = (bf16[1024,192]{0,1:T(8,128)(2,1)S(1)}, bf16[1024,192]{0,1:T(8,128)(2,1)S(1)}, u32[]{:S(2)}, u32[]{:S(2)}) collective-permute-start(bf16[1024,192]{0,1:T(8,128)(2,1)S(1)} %bitcast.332), channel_id=1, source_target_pairs={{8,0},{12,4},{16,8},{20,12},{24,16},{28,20},{9,1},{13,5},{17,9},{2... | collective-permute-start | bytes 1179656 | tf_op jit(solution)/shard_map/ppermute | solution.py:18
  975.8 22.4 %collective-permute-start.11 = (bf16[1024,192]{0,1:T(8,128)(2,1)}, bf16[1024,192]{0,1:T(8,128)(2,1)}, u32[]{:S(2)}, u32[]{:S(2)}) collective-permute-start(bf16[1024,192]{0,1:T(8,128)(2,1)} %bitcast.18), channel_id=1, source_target_pairs={{12,0},{16,4},{20,8},{24,12},{28,16},{13,1},{17,5},{21,9},{25,13},... | collective-permute-start | bytes 1179656 | tf_op jit(solution)/shard_map/ppermute | solution.py:18
  977.3 20.9 %collective-permute-start.9 = (bf16[1024,192]{0,1:T(8,128)(2,1)}, bf16[1024,192]{0,1:T(8,128)(2,1)}, u32[]{:S(2)}, u32[]{:S(2)}) collective-permute-start(bf16[1024,192]{0,1:T(8,128)(2,1)} %bitcast.16), channel_id=1, source_target_pairs={{4,0},{8,4},{12,8},{16,12},{20,16},{24,20},{28,24},{5,1},{9,5},{13... | collective-permute-start | bytes 1179656 | tf_op jit(solution)/shard_map/ppermute | solution.py:18
  981.2 22.7 %collective-permute-start.10 = (bf16[1024,192]{0,1:T(8,128)(2,1)}, bf16[1024,192]{0,1:T(8,128)(2,1)}, u32[]{:S(2)}, u32[]{:S(2)}) collective-permute-start(bf16[1024,192]{0,1:T(8,128)(2,1)} %bitcast.17), channel_id=1, source_target_pairs={{8,0},{12,4},{16,8},{20,12},{24,16},{28,20},{9,1},{13,5},{17,9},{2... | collective-permute-start | bytes 1179656 | tf_op jit(solution)/shard_map/ppermute | solution.py:18
  995.8 89.4 %reduce-scatter.24.cloned.1.call-start = ((), (), s32[]{:S(2)}) async-start(), calls=%async_computation.26 | async-start | bytes 884736 | tf_op jit(solution)/shard_map/reduce_scatter | solution.py:312
  1008.1 117.2 %reduce-scatter.26.cloned.1.call-start = ((), (), s32[]{:S(2)}) async-start(), calls=%async_computation.27 | async-start | bytes 1327104 | tf_op jit(solution)/shard_map/reduce_scatter | solution.py:315
  1013.2 152.2 %reduce-scatter.20.cloned.1.call-start = ((), (), s32[]{:S(2)}) async-start(), calls=%async_computation.24 | async-start | bytes 1327104 | tf_op jit(solution)/shard_map/reduce_scatter | solution.py:306
  1022.2 205.7 %reduce-scatter.18.cloned.1.call-start = ((), (), s32[]{:S(2)}) async-start(), calls=%async_computation.23 | async-start | bytes 3932160 | tf_op jit(solution)/shard_map/reduce_scatter | solution.py:298
  (52 other events, 4722.0 us)
Sparse Core Ops, SparseCore 0:
  31.9 62.8 all-gather.9
  96.7 43.1 all-gather.11
  141.7 24.9 all-gather.13
  260.8 66.9 reduce-scatter.11
  329.6 32.3 all-gather.19
  363.9 63.4 all-gather.15
  429.4 30.9 all-gather.17
  461.9 63.4 all-gather.23
  527.4 30.9 all-gather.21
  577.1 60.2 reduce-scatter.13
  639.7 60.2 reduce-scatter.15
  705.8 63.5 all-gather.25
  772.7 44.8 reduce-scatter.31
  821.2 46.2 reduce-scatter.29
  870.8 46.1 reduce-scatter.27
  995.9 50.8 reduce-scatter.21
  1050.1 34.9 reduce-scatter.23
  1088.5 36.7 reduce-scatter.25
  1128.6 36.7 reduce-scatter.19
  1167.6 60.2 reduce-scatter.17
where the time goes:
time: 1290 us; the launch traced here: 1280 us
  waiting for transfers between devices  701 us (54%)
  matrix products  308 us (24%)
  other arithmetic  91 us (7%)
  blocking collectives  78.3 us (6%)
  local copies, waits for them, and re-layouts  61.1 us (5%)
  starting transfers between devices  25.5 us (2%)
  between operations  16 us (1%)
    reduce_scatter x1, waiting for transfers between devices, per_device(): lax.psum_scatter(attn_part.astype(jnp.bfloat16), 'tensor', scatter_dimens...  66.5 us
    all_gather x1, waiting for transfers between devices, per_device(): lax.all_gather(normed_two.astype(jnp.bfloat16), 'tensor', axis=0, tiled=T...  65.5 us
    reduce_scatter x1, waiting for transfers between devices, per_device(): lax.psum_scatter(grad_two_rows.astype(jnp.bfloat16), 'tensor', scatter_di...  62.6 us
    reduce_scatter x1, waiting for transfers between devices, per_device(): lax.psum_scatter(grad_one_rows.astype(jnp.bfloat16), 'tensor', scatter_di...  60.9 us
    dot_general x4, matrix products, block_scores(): jnp.einsum('qgrd,kgd->grqk', query_block, keys_all, preferred_element_typ...  60 us
    all_gather x1, waiting for transfers between devices, per_device(): grad_rows_ffn = lax.all_gather(grad_out, 'tensor', axis=0, tiled=True)  56.9 us
    reduce_scatter x1, waiting for transfers between devices, per_device(): lax.psum_scatter(ffn_part.astype(jnp.bfloat16), 'tensor', scatter_dimensi...  49.2 us
    dot_general x2, matrix products, attend_back(): jnp.einsum('qgrd,kgd->grqk', grad_weighted, values_all, preferred_element...  43.6 us
  transfers between devices with their start and end apart: 32, of which 21 were waited for; matrix products, arithmetic and copies ran while one was open for 32% of the time, Pallas kernels for 0%

commit v1 on v0

v1 whole, which is shorter than its diff:
```python
import functools
import jax
import jax.numpy as jnp
from jax import lax
from jax.experimental import pallas as pl
from jax.experimental.pallas import tpu as pltpu
from jax.sharding import Mesh, PartitionSpec as P

HEAD = 96
LANES = 128
SEQUENCE_LENGTH = 4096
SPANS = 4
EPSILON = 1e-05
ROPE_BASE = 100000.0
MASKED = -1e30
LOG2E = 1.4426950408889634
NT = (((1,), (1,)), ((), ()))
NN = (((1,), (0,)), ((), ()))
TN = (((0,), (0,)), ((), ()))
F32 = jnp.float32
BF16 = jnp.bfloat16
VMEM_LIMIT = 60 * 1024 * 1024


def mm(left, right, dims):
    return lax.dot_general(left, right, dims, preferred_element_type=F32)


def widen(piece):
    return jnp.concatenate([piece, jnp.zeros((piece.shape[0], LANES - HEAD), piece.dtype)], axis=1)


def swapped(value):
    half = HEAD // 2
    return jnp.concatenate([value[:, half:HEAD], value[:, :half]], axis=1)


def attend_kernel(ids, own0, own1, own2, own3, other, out0, out1, out2, out3, q_s, kv_s, o_s, lse_s, acc_s, vt_s, *, block, tile):
    z, t = ids[0], ids[1]
    c = lax.rem(t, 2)
    spans = 4
    rows_all = q_s.shape[0]
    for j, own in enumerate((own0, own1, own2, own3)):
        zj = z ^ j
        for r in range(spans):
            at = pl.multiple_of(((t ^ r) * spans + zj) * block, block)
            at_other = pl.multiple_of(((t ^ 1 ^ r) * spans + zj) * block, block)
            q_s[pl.ds(at, block), :] = widen(own[:, r * HEAD : (r + 1) * HEAD])
            kv_s[c, pl.ds(at, block), :] = widen(own[:, (spans + r) * HEAD : (spans + r + 1) * HEAD])
            kv_s[1 - c, pl.ds(at_other, block), :] = widen(other[j, :, r * HEAD : (r + 1) * HEAD])
    factor = HEAD ** (-0.5) * LOG2E
    is_count = lax.broadcasted_iota(jnp.int32, (tile, LANES), 1) == HEAD

    def values(i, _):
        rows = pl.ds(pl.multiple_of(i * tile, tile), tile)
        vals = kv_s[1, rows, :]
        vt_s[:, rows] = jnp.transpose(jnp.where(is_count, jnp.ones_like(vals), vals))
        return 0

    lax.fori_loop(0, rows_all // tile, values, 0)

    def step(query, j, before, mask):
        rows = pl.ds(pl.multiple_of(j * tile, tile), tile)
        scores = mm(kv_s[0, rows, :], query, NT) * factor
        if mask is not None:
            scores = jnp.where(mask, scores, MASKED)
        top = jnp.maximum(before, jnp.max(scores, axis=0, keepdims=True))
        expo = jnp.exp2(scores - top).astype(BF16)
        acc_s[...] = acc_s[...] * jnp.exp2(before - top) + mm(vt_s[:, rows], expo, NN)
        return top

    def row_block(i, _):
        at = pl.multiple_of(i * tile, tile)
        query = q_s[pl.ds(at, tile), :]
        acc_s[...] = jnp.zeros_like(acc_s)
        top = lax.fori_loop(0, i, lambda j, top: step(query, j, top, None), jnp.full((1, tile), MASKED, F32))
        mask = lax.broadcasted_iota(jnp.int32, (tile, tile), 0) <= lax.broadcasted_iota(jnp.int32, (tile, tile), 1)
        top = step(query, i, top, mask)
        acc = acc_s[...]
        denom = acc[HEAD : HEAD + 1, :]
        o_s[pl.ds(at, tile), :] = jnp.transpose(acc / denom).astype(BF16)
        lse_s[:, pl.ds(at, tile)] = jnp.broadcast_to(top + jnp.log2(denom), (8, tile))
        return 0

    lax.fori_loop(0, rows_all // tile, row_block, 0)
    for j, out in enumerate((out0, out1, out2, out3)):
        zj = z ^ j
        for r in range(spans):
            at = pl.multiple_of(((t ^ r) * spans + zj) * block, block)
            out[:, r * HEAD : (r + 1) * HEAD] = o_s[pl.ds(at, block), :HEAD]


VM = pl.BlockSpec(memory_space=pltpu.VMEM)
SM = pl.BlockSpec(memory_space=pltpu.SMEM)


def shape(dims, dtype=BF16):
    return jax.ShapeDtypeStruct(dims, dtype)


def params():
    return pltpu.CompilerParams(vmem_limit_bytes=VMEM_LIMIT)


def attend(ids, own, other, tile=1024):
    block = own[0].shape[0]
    rows = block * 16
    return pl.pallas_call(
        functools.partial(attend_kernel, block=block, tile=tile),
        out_shape=[shape((block, 4 * HEAD))] * 4
        + [shape((rows, LANES)), shape((2, rows, LANES)), shape((rows, LANES)), shape((8, rows), F32)],
        in_specs=[SM] + [VM] * 5,
        out_specs=[VM] * 8,
        scratch_shapes=[pltpu.VMEM((LANES, tile), F32), pltpu.VMEM((LANES, rows), BF16)],
        compiler_params=params(),
        cost_estimate=pl.CostEstimate(flops=int(8e9), bytes_accessed=int(8e6), transcendentals=int(9e6)),
        name="attend",
    )(ids, *own, other)


def attend_back_kernel(ids, q_s, kv_s, o_s, lse_s, cos_s, sin_s, g0, g1, g2, g3, dq0, dq1, dq2, dq3, dk_out, dv_out, g_s, qx_s, kx_s, delta_s, dq_s, dk_s, dv_s, *, block, tile):
    z, t = ids[0], ids[1]
    spans = 4
    rows_all = q_s.shape[0]
    tiles = rows_all // tile
    for j, piece in enumerate((g0, g1, g2, g3)):
        zj = z ^ j
        for r in range(spans):
            at = pl.multiple_of(((t ^ r) * spans + zj) * block, block)
            g_s[pl.ds(at, block), :] = widen(piece[:, r * HEAD : (r + 1) * HEAD])

    def prepare(i, _):
        at = pl.multiple_of(i * tile, tile)
        rows = pl.ds(at, tile)
        query = q_s[rows, :]
        keys = kv_s[0, rows, :]
        qx_s[rows, :LANES] = query
        qx_s[rows, LANES:] = widen(swapped(query))
        kx_s[rows, :LANES] = keys
        kx_s[rows, LANES:] = widen(swapped(keys))
        both = g_s[rows, :].astype(F32) * o_s[rows, :].astype(F32)
        delta = jnp.sum(both, axis=1, keepdims=True)
        delta_s[:, rows] = jnp.transpose(jnp.broadcast_to(delta, (tile, LANES)))[:8]
        dq_s[rows, :] = jnp.zeros((tile, 2 * LANES), F32)
        return 0

    lax.fori_loop(0, tiles, prepare, 0)
    factor = HEAD ** (-0.5) * LOG2E
    scale = HEAD ** (-0.5)

    def step(i, keys, vals, kx, mask):
        rows = pl.ds(pl.multiple_of(i * tile, tile), tile)
        query = qx_s[rows, :]
        grad = g_s[rows, :]
        scores = mm(keys, query[:, :LANES], NT) * factor - lse_s[:1, rows]
        if mask is not None:
            scores = jnp.where(mask, scores, MASKED)
        prob = jnp.exp2(scores)
        through = mm(vals, grad, NT)
        ds = (prob * (through - delta_s[:1, rows])).astype(BF16)
        dv_s[...] += mm(prob.astype(BF16), grad, NN)
        dk_s[...] += mm(ds, query, NN)
        dq_s[rows, :] += mm(ds, kx, TN)

    def column_block(j, _):
        rows = pl.ds(pl.multiple_of(j * tile, tile), tile)
        kx = kx_s[rows, :]
        keys = kx[:, :LANES]
        vals = kv_s[1, rows, :]
        dk_s[...] = jnp.zeros_like(dk_s)
        dv_s[...] = jnp.zeros_like(dv_s)
        mask = lax.broadcasted_iota(jnp.int32, (tile, tile), 0) <= lax.broadcasted_iota(jnp.int32, (tile, tile), 1)
        step(j, keys, vals, kx, mask)
        lax.fori_loop(j + 1, tiles, lambda i, _: (step(i, keys, vals, kx, None), 0)[1], 0)
        dk = dk_s[...] * scale
        dk_out[rows, :] = (dk[:, :LANES] * cos_s[rows, :] - dk[:, LANES:] * sin_s[rows, :]).astype(BF16)
        dv_out[rows, :] = dv_s[...].astype(BF16)
        return 0

    lax.fori_loop(0, tiles, column_block, 0)
    for j, out in enumerate((dq0, dq1, dq2, dq3)):
        zj = z ^ j
        for r in range(spans):
            rows = pl.ds(pl.multiple_of(((t ^ r) * spans + zj) * block, block), block)
            dq = dq_s[rows, :] * scale
            out[:, r * HEAD : (r + 1) * HEAD] = (
                dq[:, :LANES] * cos_s[rows, :] - dq[:, LANES:] * sin_s[rows, :]
            ).astype(BF16)[:, :HEAD]


def attend_back(ids, q, kv, o, lse, cosine, sine, grads, tile=1024):
    block = grads[0].shape[0]
    rows = block * 16
    return pl.pallas_call(
        functools.partial(attend_back_kernel, block=block, tile=tile),
        out_shape=[shape((block, 4 * HEAD))] * 4 + [shape((rows, LANES))] * 2,
        in_specs=[SM] + [VM] * 10,
        out_specs=[VM] * 6,
        scratch_shapes=[
            pltpu.VMEM((rows, LANES), BF16),
            pltpu.VMEM((rows, 2 * LANES), BF16),
            pltpu.VMEM((rows, 2 * LANES), BF16),
            pltpu.VMEM((8, rows), F32),
            pltpu.VMEM((rows, 2 * LANES), F32),
            pltpu.VMEM((tile, 2 * LANES), F32),
            pltpu.VMEM((tile, LANES), F32),
        ],
        compiler_params=params(),
        cost_estimate=pl.CostEstimate(flops=int(22e9), bytes_accessed=int(12e6), transcendentals=int(9e6)),
        name="attend_back",
    )(ids, q, kv, o, lse, cosine, sine, *grads)


def project_kernel(ids, x0, x1, x2, x3, a, cos_s, sin_s, *outs, block):
    z, t = ids[0], ids[1]
    is_value = lax.rem(t, 2) == 1
    for j, out in enumerate(outs):
        weights = a[z ^ j, : 2 * HEAD, :]
        for r, x in enumerate((x0, x1, x2, x3)):
            rows = pl.ds(pl.multiple_of(((t ^ r) * SPANS + z) * block, block), block)
            cosine, sine = cos_s[rows, :HEAD], sin_s[rows, :HEAD]
            made = mm(x[...], weights, NT)
            query, other = made[:, :HEAD], made[:, HEAD:]
            out[:, r * HEAD : (r + 1) * HEAD] = (query * cosine + swapped(query) * sine).astype(BF16)
            cosine = jnp.where(is_value, 1.0, cosine)
            sine = jnp.where(is_value, 0.0, sine)
            out[:, (SPANS + r) * HEAD : (SPANS + r + 1) * HEAD] = (
                other * cosine + swapped(other) * sine
            ).astype(BF16)


def project(ids, x, a, cosine, sine):
    block = x[0].shape[0]
    return pl.pallas_call(
        functools.partial(project_kernel, block=block),
        out_shape=[shape((block, 8 * HEAD))] * 4,
        in_specs=[SM] + [VM] * 7,
        out_specs=[VM] * 4,
        compiler_params=params(),
        cost_estimate=pl.CostEstimate(flops=int(3e9), bytes_accessed=int(10e6), transcendentals=0),
        name="project",
    )(ids, *x, a, cosine, sine)


def gathered_heads(pieces, att, block):
    for j, piece in enumerate(pieces):
        for r in range(SPANS):
            att[r * block : (r + 1) * block, j * HEAD : (j + 1) * HEAD] = piece[:, r * HEAD : (r + 1) * HEAD]


def out_kernel(ids, p0, p1, p2, p3, a, near, far, att, orel, *, block):
    z = ids[0]
    gathered_heads((p0, p1, p2, p3), att, block)
    for j in range(4):
        orel[j * HEAD : (j + 1) * HEAD, :] = a[z ^ j, 2 * HEAD :, :]
    for r in range(SPANS):
        made = mm(att[r * block : (r + 1) * block, :], orel[...], NN).astype(BF16)
        (far if r % 2 else near)[r // 2] = made


def out_project(ids, pieces, a):
    block, width = pieces[0].shape[0], a.shape[2]
    return pl.pallas_call(
        functools.partial(out_kernel, block=block),
        out_shape=[shape((2, block, width))] * 2 + [shape((4 * block, 4 * HEAD)), shape((4 * HEAD, width))],
        in_specs=[SM] + [VM] * 5,
        out_specs=[VM] * 4,
        compiler_params=params(),
        cost_estimate=pl.CostEstimate(flops=int(1.3e9), bytes_accessed=int(10e6), transcendentals=0),
        name="out_project",
    )(ids, *pieces, a)


def out_back_kernel(ids, g0, g1, g2, g3, att, orel, d0, d1, d2, d3, dout, *, block):
    z = ids[0]
    grads = (g0, g1, g2, g3)
    for r, grad in enumerate(grads):
        made = mm(grad[...], orel[...], NT).astype(BF16)
        for j, out in enumerate((d0, d1, d2, d3)):
            out[:, r * HEAD : (r + 1) * HEAD] = made[:, j * HEAD : (j + 1) * HEAD]
    total = None
    for r, grad in enumerate(grads):
        made = mm(att[r * block : (r + 1) * block, :], grad[...], TN)
        total = made if total is None else total + made
    for j in range(4):
        dout[z ^ j] = total[j * HEAD : (j + 1) * HEAD].astype(BF16)


def out_back(ids, grads, att, orel):
    block, width = grads[0].shape
    return pl.pallas_call(
        functools.partial(out_back_kernel, block=block),
        out_shape=[shape((block, 4 * HEAD))] * 4 + [shape((4, HEAD, width))],
        in_specs=[SM] + [VM] * 6,
        out_specs=[VM] * 5,
        compiler_params=params(),
        cost_estimate=pl.CostEstimate(flops=int(2.5e9), bytes_accessed=int(10e6), transcendentals=0),
        name="out_back",
    )(ids, *grads, att, orel)


def pack_kernel(ids, mine, theirs, k0, k1, k2, k3, *, block):
    z, t = ids[0], ids[1]
    for j, out in enumerate((k0, k1, k2, k3)):
        for r in range(SPANS):
            rows = pl.ds(pl.multiple_of(((t ^ r) * SPANS + (z ^ j)) * block, block), block)
            total = (mine[rows, :].astype(F32) + theirs[rows, :].astype(F32)).astype(BF16)
            out[:, r * HEAD : (r + 1) * HEAD] = total[:, :HEAD]


def pack(ids, mine, theirs):
    block = mine.shape[0] // 16
    return pl.pallas_call(
        functools.partial(pack_kernel, block=block),
        out_shape=[shape((block, 4 * HEAD))] * 4,
        in_specs=[SM] + [VM] * 2,
        out_specs=[VM] * 4,
        compiler_params=params(),
        cost_estimate=pl.CostEstimate(flops=int(1e6), bytes_accessed=int(3e6), transcendentals=0),
        name="pack",
    )(ids, mine, theirs)


def project_back_kernel(ids, q0, q1, q2, q3, k0, k1, k2, k3, x0, x1, x2, x3, a, near, far, da, d_s, a_s, *, block):
    z = ids[0]
    for j, (query, other) in enumerate(zip((q0, q1, q2, q3), (k0, k1, k2, k3))):
        for r in range(SPANS):
            rows = slice(r * block, (r + 1) * block)
            lanes = slice(r * HEAD, (r + 1) * HEAD)
            d_s[rows, 2 * j * HEAD : (2 * j + 1) * HEAD] = query[:, lanes]
            d_s[rows, (2 * j + 1) * HEAD : (2 * j + 2) * HEAD] = other[:, lanes]
        a_s[2 * j * HEAD : (2 * j + 2) * HEAD, :] = a[z ^ j, : 2 * HEAD, :]
    for r in range(SPANS):
        made = mm(d_s[r * block : (r + 1) * block, :], a_s[...], NN).astype(BF16)
        (far if r % 2 else near)[r // 2] = made
    total = None
    for r, x in enumerate((x0, x1, x2, x3)):
        made = mm(d_s[r * block : (r + 1) * block, :], x[...], TN)
        total = made if total is None else total + made
    for j in range(4):
        da[z ^ j] = total[2 * j * HEAD : (2 * j + 2) * HEAD].astype(BF16)


def project_back(ids, queries, others, x, a):
    block, width = x[0].shape
    return pl.pallas_call(
        functools.partial(project_back_kernel, block=block),
        out_shape=[shape((2, block, width))] * 2 + [shape((4, 2 * HEAD, width))],
        in_specs=[SM] + [VM] * 13,
        out_specs=[VM] * 3,
        scratch_shapes=[pltpu.VMEM((4 * block, 8 * HEAD), BF16), pltpu.VMEM((8 * HEAD, width), BF16)],
        compiler_params=params(),
        cost_estimate=pl.CostEstimate(flops=int(5e9), bytes_accessed=int(14e6), transcendentals=0),
        name="project_back",
    )(ids, *queries, *others, *x, a)


def swap(value, axis):
    return lax.ppermute(value, axis, [(0, 1), (1, 0)])


def gather_group(value):
    core = swap(value, "c")
    across = swap(value, "x")
    return value, core, across, swap(across, "c")


def scatter_group(near, far):
    total = near.astype(F32) + swap(far, "c").astype(F32)
    return total[0] + swap(total[1].astype(BF16), "x").astype(F32)


def exchange(pieces):
    count = lax.axis_size("z")
    return [pieces[0]] + [
        lax.ppermute(pieces[j], "z", [(i, i ^ j) for i in range(count)]) for j in range(1, count)
    ]


def unit(values):
    scale = lax.rsqrt(jnp.mean(values * values, axis=-1, keepdims=True) + EPSILON)
    return values * scale, scale


def unit_back(values, scale, grad):
    inner = jnp.mean(grad * values, axis=-1, keepdims=True)
    return scale * grad - values * (scale * scale * scale) * inner


def spread(payload):
    return lax.all_to_all(payload, ("x", "c"), split_axis=0, concat_axis=0, tiled=True)


def per_device(tokens, w_query, w_key, w_value, w_out, w_gate, w_up, w_down, norm_attn, norm_ffn, grad_out):
    sequences, count = lax.axis_size("y"), lax.axis_size("z")
    block, width = tokens.shape
    shard = w_query.shape[0]
    part = SPANS * shard
    z = lax.axis_index("z")
    t = lax.axis_index("x") * 2 + lax.axis_index("c")
    ids = jnp.stack([z, t]).astype(jnp.int32)
    rows_all = SEQUENCE_LENGTH
    units = w_gate.shape[1] // SPANS

    gain_attn = norm_attn.astype(F32)[:, None]
    gain_ffn = norm_ffn.astype(F32)[:, None]
    scaled_query = (w_query.astype(F32) * gain_attn).astype(BF16)
    scaled_key = (w_key.astype(F32) * gain_attn).astype(BF16)
    scaled_value = (w_value.astype(F32) * gain_attn).astype(BF16)
    scaled_gate = (w_gate.astype(F32) * gain_ffn).astype(BF16)
    scaled_up = (w_up.astype(F32) * gain_ffn).astype(BF16)

    by_query = scaled_query.T.reshape(SPANS, HEAD, shard)
    by_key = scaled_key.T.reshape(2, HEAD, shard)
    by_value = scaled_value.T.reshape(2, HEAD, shard)
    by_kv = jnp.stack([by_key[0], by_value[0], by_key[1], by_value[1]])
    payload = jnp.concatenate([by_query, by_kv, w_out.reshape(SPANS, HEAD, shard)], axis=1)
    payload = spread(payload).transpose(1, 0, 2).reshape(3 * HEAD, part)
    attn_weights = lax.all_gather(payload, ("y", "z"), axis=0, tiled=False)
    attn_weights = attn_weights.reshape(sequences, count, 3 * HEAD, part).transpose(1, 2, 0, 3)
    attn_weights = attn_weights.reshape(count, 3 * HEAD, width)

    resid = tokens.astype(F32)
    unit_one, scale_one = unit(resid)
    x_one = gather_group(unit_one.astype(BF16))

    payload = jnp.stack(
        [
            scaled_gate.reshape(shard, SPANS, units).transpose(1, 0, 2),
            scaled_up.reshape(shard, SPANS, units).transpose(1, 0, 2),
            w_down.T.reshape(shard, SPANS, units).transpose(1, 0, 2),
        ],
        axis=1,
    )
    payload = spread(payload).transpose(1, 0, 2, 3).reshape(3, part, units)
    ffn_weights = lax.all_gather(payload, ("y", "z"), axis=0, tiled=False)
    ffn_weights = ffn_weights.reshape(sequences, count, 3, part, units).transpose(2, 0, 3, 1, 4)
    ffn_weights = ffn_weights.reshape(3, width, count * units)
    grad_rows = jnp.concatenate(gather_group(grad_out), axis=0)

    lane = jnp.arange(LANES)
    angle = jnp.arange(rows_all, dtype=F32)[:, None] * (ROPE_BASE ** (-(lane % (HEAD // 2) * 2.0) / HEAD))[None, :]
    cosine = jnp.cos(angle)
    sine = jnp.sin(angle) * jnp.where(lane < HEAD // 2, -1.0, 1.0)

    made = project(ids, x_one, attn_weights, cosine, sine)
    made = exchange(made)
    other = swap(jnp.stack([piece[:, SPANS * HEAD :] for piece in made]), "c")
    *attended, q_seq, kv_seq, o_seq, lse = attend(ids, made, other)
    near, far, att, orel = out_project(ids, exchange(attended), attn_weights)
    branch_attn = scatter_group(near, far)
    state = resid + branch_attn
    unit_two, scale_two = unit(state)
    x_two = jnp.concatenate(gather_group(unit_two.astype(BF16)), axis=0)

    full_gate, full_up, full_down = ffn_weights
    gate = jnp.dot(x_two, full_gate, preferred_element_type=F32)
    up = jnp.dot(x_two, full_up, preferred_element_type=F32)
    sigma = jax.nn.sigmoid(gate)
    swish = gate * sigma
    hidden = (swish * up).astype(BF16)
    ffn_part = mm(hidden, full_down, NT).astype(BF16).reshape(SPANS, block, width)
    branch_ffn = scatter_group(ffn_part[0::2], ffn_part[1::2])
    result = state + branch_ffn

    grad_hidden = jnp.dot(grad_rows, full_down, preferred_element_type=F32)
    grad_gate_pre = (grad_hidden * up * (sigma * (1.0 + gate * (1.0 - sigma)))).astype(BF16)
    grad_up_pre = (grad_hidden * swish).astype(BF16)
    two_part = (mm(grad_gate_pre, full_gate, NT) + mm(grad_up_pre, full_up, NT)).astype(BF16)
    two_part = two_part.reshape(SPANS, block, width)
    grad_unit_two = scatter_group(two_part[0::2], two_part[1::2])
    grad_state = grad_out.astype(F32) + unit_back(state, scale_two, grad_unit_two)

    def settle(grads):
        grads = grads.reshape(3, sequences, part, count, units).transpose(1, 3, 0, 2, 4)
        grads = grads.reshape(sequences * count, 3, part, units)
        total = lax.psum_scatter(grads, ("y", "z"), scatter_dimension=0, tiled=False)
        total = spread(total.reshape(3, SPANS, shard, units).transpose(1, 0, 2, 3))
        return total.transpose(1, 2, 0, 3).reshape(3, shard, SPANS * units).astype(F32)

    grad_ffn = settle(
        jnp.stack(
            [
                mm(x_two, grad_gate_pre, TN).astype(BF16),
                mm(x_two, grad_up_pre, TN).astype(BF16),
                mm(grad_rows, hidden, TN).astype(BF16),
            ]
        )
    )

    g_state = gather_group(grad_state.astype(BF16))
    *grad_att, grad_out_w = out_back(ids, g_state, att, orel)
    *dq, dk, dv = attend_back(ids, q_seq, kv_seq, o_seq, lse, cosine, sine, exchange(grad_att))
    dq = exchange(dq)
    first = lax.axis_index("c") == 0
    keep, give = jnp.where(first, dk, dv), jnp.where(first, dv, dk)
    dkv = exchange(pack(ids, keep, swap(give, "c")))
    near, far, grad_qkv = project_back(ids, dq, dkv, x_one, attn_weights)
    grad_unit_one = scatter_group(near, far)
    grad_tokens = (grad_state + unit_back(resid, scale_one, grad_unit_one)).astype(BF16)

    grads = jnp.concatenate([grad_qkv, grad_out_w], axis=1)
    grads = grads.reshape(count, 3 * HEAD, sequences, part).transpose(2, 0, 1, 3)
    grads = grads.reshape(sequences * count, 3 * HEAD, part)
    total = lax.psum_scatter(grads, ("y", "z"), scatter_dimension=0, tiled=False)
    total = spread(total.reshape(3 * HEAD, SPANS, shard).transpose(1, 0, 2)).astype(F32)
    grad_query = total[:, :HEAD].reshape(SPANS * HEAD, shard).T
    grad_key = total[0::2, HEAD : 2 * HEAD].reshape(2 * HEAD, shard).T
    grad_value = total[1::2, HEAD : 2 * HEAD].reshape(2 * HEAD, shard).T
    grad_outproj = total[:, 2 * HEAD :].reshape(SPANS * HEAD, shard)

    gain_one = (
        jnp.sum(w_query.astype(F32) * grad_query, axis=1)
        + jnp.sum(w_key.astype(F32) * grad_key, axis=1)
        + jnp.sum(w_value.astype(F32) * grad_value, axis=1)
    )
    gain_two = jnp.sum(w_gate.astype(F32) * grad_ffn[0], axis=1) + jnp.sum(w_up.astype(F32) * grad_ffn[1], axis=1)
    gain_one, gain_two = lax.psum((gain_one, gain_two), "z")

    squares = jnp.stack([jnp.sum(result * result), jnp.sum(branch_attn * branch_attn), jnp.sum(branch_ffn * branch_ffn)])
    squares = lax.psum(squares, ("y", "x", "c", "z"))
    entries = block * width * sequences * SPANS * count
    return (
        result.astype(BF16),
        grad_tokens,
        grad_query * gain_attn,
        grad_key * gain_attn,
        grad_value * gain_attn,
        grad_outproj,
        grad_ffn[0] * gain_ffn,
        grad_ffn[1] * gain_ffn,
        grad_ffn[2].T,
        gain_one,
        gain_two,
        jnp.sqrt(squares / entries),
    )


def solution(mesh):
    fsdp, tensor = mesh.shape["fsdp"], mesh.shape["tensor"]
    split = Mesh(mesh.devices.reshape(fsdp // SPANS, 2, 2, tensor), ("y", "x", "c", "z"))
    rows = ("y", "x", "c")
    tok = P(("y", "x", "c", "z"), None)
    col, row, vec = P(rows, "z"), P("z", rows), P(rows)
    return jax.shard_map(
        per_device,
        mesh=split,
        in_specs=(tok, col, col, col, row, col, col, row, vec, vec, tok),
        out_specs=(tok, tok, col, col, col, row, col, col, row, vec, vec, P()),
        check_vma=False,
    )
```

time: 1290 us -> 845 us (0.66)
  waiting for transfers between devices: 701 us -> 398 us
  matrix products: 308 us -> 49.9 us
  Pallas kernels: 0 us -> 97.1 us
  other arithmetic: 91 us -> 42.7 us
  starting transfers between devices: 25.5 us -> 58.6 us
  local copies, waits for them, and re-layouts: 61.1 us -> 83.4 us
  blocking collectives: 78.3 us -> 93.9 us
    all_gather x9 -> x2, waiting for transfers between devices: 311 us -> 13.7 us  [the longest x1 13.7 us: per_device(): attn_weights = lax.all_gather(payload, ('y', 'z'), axis=0, tiled=False)]
    dot_general x35 -> x9, matrix products: 308 us -> 49.9 us  [the longest x6 30.7 us: mm(): return lax.dot_general(left, right, dims, preferred_element_type=F32)]
    reduce_scatter x11 -> x2, waiting for transfers between devices: 362 us -> 115 us  [the longest x1 115 us: settle(): lax.psum_scatter(grads, ('y', 'z'), scatter_dimension=0, tiled=False)]
    ppermute x12 -> x37, waiting for transfers between devices: 23.9 us -> 251 us  [the longest x22 126 us: swap(): return lax.ppermute(value, axis, [(0, 1), (1, 0)])]
    pallas_call x0 -> x7, Pallas kernels: none -> 97.1 us  [the longest x1 38.9 us: attend_back(): pl.pallas_call(functools.partial(attend_back_kernel, block=block, tile=ti...]
    another operation x0 -> x14, local copies, waits for them, and re-layouts: none -> 33.7 us  [the longest x6 25.8 us: per_device(): jnp.stack([mm(x_two, grad_gate_pre, TN).astype(BF16), mm(x_two, grad_up_p...]
    reduce_sum x8 -> x7, other arithmetic: 41.4 us -> 8.06 us  [the longest x1 2.11 us: per_device(): jnp.sum(result * result)]
    all_to_all x0 -> x2, blocking collectives: none -> 32.1 us  [spread(): lax.all_to_all(payload, ('x', 'c'), split_axis=0, concat_axis=0, tiled=True)]
  transfers between devices with their start and end apart: 32 -> 43, of which waited for: 21 -> 26; matrix products, arithmetic and copies ran while one was open for 32% -> 14% of each run, Pallas kernels for 0% -> 5%
where the time goes in v1:
time: 845 us; the launch traced here: 839 us
  waiting for transfers between devices  398 us (47%)
  Pallas kernels  97.1 us (11%)
  blocking collectives  93.9 us (11%)
  local copies, waits for them, and re-layouts  83.4 us (10%)
  starting transfers between devices  58.6 us (7%)
  matrix products  49.9 us (6%)
  other arithmetic  42.7 us (5%)
  between operations  14.9 us (2%)
    ppermute x22, waiting for transfers between devices, swap(): return lax.ppermute(value, axis, [(0, 1), (1, 0)])  126 us
    ppermute x15, waiting for transfers between devices, exchange(): lax.ppermute(pieces[j], 'z', [(i, i ^ j) for i in range(count)])  125 us
    reduce_scatter x1, waiting for transfers between devices, settle(): lax.psum_scatter(grads, ('y', 'z'), scatter_dimension=0, tiled=False)  115 us
    psum x1, blocking collectives, per_device(): squares = lax.psum(squares, ('y', 'x', 'c', 'z'))  51.7 us
    ppermute x15, starting transfers between devices, exchange(): lax.ppermute(pieces[j], 'z', [(i, i ^ j) for i in range(count)])  39.4 us
    pallas_call x1, Pallas kernels, attend_back(): pl.pallas_call(functools.partial(attend_back_kernel, block=block, tile=ti...  38.9 us
    all_to_all x2, blocking collectives, spread(): lax.all_to_all(payload, ('x', 'c'), split_axis=0, concat_axis=0, tiled=True)  32.1 us
    dot_general x6, matrix products, mm(): return lax.dot_general(left, right, dims, preferred_element_type=F32)  30.7 us
  transfers between devices with their start and end apart: 43, of which 26 were waited for; matrix products, arithmetic and copies ran while one was open for 14% of the time, Pallas kernels for 5%

profile of v1, /device:TPU:0, one launch (start us, length us, event | category | flops | bytes accessed | tf_op | source)
XLA Modules:
  0.0 838.8 jit_solution(8574855908281886911)
XLA Ops:
  14.8 13.7 %all_to_all.20 = bf16[4,288,192]{1,2,0:T(8,128)(2,1)S(1)} all-to-all(bf16[4,288,192]{1,2,0:T(8,128)(2,1)S(1)} %copy.123), channel_id=1, replica_groups=mesh['y'=2,'x'=2,'c'=2,'z'=4] {'x','c'}, dimensions={0} | all-to-all | bytes 884736 | tf_op jit(solution)/shard_map/all_to_all | solution.py:391
  32.2 18.4 %all_to_all.21 = bf16[4,3,192,256]{3,2,1,0:T(8,128)(2,1)S(1)} all-to-all(bf16[4,3,192,256]{3,2,1,0:T(8,128)(2,1)S(1)} %copy.126), channel_id=1, replica_groups=mesh['y'=2,'x'=2,'c'=2,'z'=4] {'x','c'}, dimensions={0} | all-to-all | bytes 2359296 | tf_op jit(solution)/shard_map/all_to_all | solution.py:391
  54.4 18.3 %collective-permute-done.1.x2 = bf16[256,1536]{1,0:T(8,128)(2,1)S(1)} collective-permute-done((bf16[256,1536]{1,0:T(8,128)(2,1)S(1)}, bf16[256,1536]{1,0:T(8,128)(2,1)S(1)}, u32[]{:S(2)}, u32[]{:S(2)}) %collective-permute-start.1) | collective-permute-done | bytes 786464 | tf_op jit(solution)/shard_map/ppermute | solution.py:359
  72.7 8.8 %sine_multiply_fusion = (f32[4096,128]{1,0:T(8,128)}, f32[4096,128]{1,0:T(8,128)}) fusion(f32[128]{0:T(128)S(1)} %compare_select_fusion, f32[128]{0:T(128)S(1)} %fusion.36), kind=kLoop, calls=%fused_computation.25 | loop fusion | flops 1048576 | bytes 4195328 | tf_op jit(solution)/shard_map/mul | solution.py:444
  81.5 13.7 %all-gather.3.cloned.1.call-done = bf16[8,288,768]{2,1,0:T(8,128)(2,1)} async-done(((bf16[1,288,768]{2,1,0:T(8,128)(2,1)}), bf16[8,288,768]{2,1,0:T(8,128)(2,1)}) %all-gather.3.cloned.1.call-update) | async-done | bytes 3538960 | tf_op jit(solution)/shard_map/all_gather | solution.py:419
  100.2 10.9 %project.1 = (bf16[256,768]{1,0:T(8,128)(2,1)}, bf16[256,768]{1,0:T(8,128)(2,1)}, bf16[256,768]{1,0:T(8,128)(2,1)}, bf16[256,768]{1,0:T(8,128)(2,1)}) custom-call(s32[2]{0:T(128)} %pad_add_fusion.ids, bf16[256,1536]{1,0:T(8,128)(2,1)} %copy-done.18, bf16[256,1536]{1,0:T(8,128)(2,1)} %copy-done.35, bf16[256,1536]{1,0:T(8,128)(2,1)} %copy-done.34, ...), custom_call_target="tpu_custom_call" | custom-call | flops 3000000000 | bytes 10000000 | tf_op jit(solution)/shard_map/project/pallas_call | solution.py:234
  116.5 17.0 %collective-permute-done.5.own3 = bf16[256,768]{1,0:T(8,128)(2,1)S(1)} collective-permute-done((bf16[256,768]{1,0:T(8,128)(2,1)}, bf16[256,768]{1,0:T(8,128)(2,1)S(1)}, u32[]{:S(2)}, u32[]{:S(2)}) %collective-permute-start.5) | collective-permute-done | bytes 393248 | tf_op jit(solution)/shard_map/ppermute | solution.py:376
  133.6 46.9 %collective-permute-done.4.own2 = bf16[256,768]{1,0:T(8,128)(2,1)S(1)} collective-permute-done((bf16[256,768]{1,0:T(8,128)(2,1)}, bf16[256,768]{1,0:T(8,128)(2,1)S(1)}, u32[]{:S(2)}, u32[]{:S(2)}) %collective-permute-start.4) | collective-permute-done | bytes 393248 | tf_op jit(solution)/shard_map/ppermute | solution.py:376
  183.9 21.9 %attend.1 = (bf16[256,384]{1,0:T(8,128)(2,1)}, bf16[256,384]{1,0:T(8,128)(2,1)}, bf16[256,384]{1,0:T(8,128)(2,1)}, bf16[256,384]{1,0:T(8,128)(2,1)}, bf16[4096,1...) custom-call(s32[2]{0:T(128)} %pad_add_fusion.ids, ...), custom_call_target="tpu_custom_call" | custom-call | flops 8000000000 | bytes 8000000 | tf_op jit(solution)/shard_map/attend/pallas_call | solution.py:108
  210.2 14.0 %collective-permute-done.7.p1 = bf16[256,384]{1,0:T(8,128)(2,1)S(1)} collective-permute-done((bf16[256,384]{1,0:T(8,128)(2,1)}, bf16[256,384]{1,0:T(8,128)(2,1)S(1)}, u32[]{:S(2)}, u32[]{:S(2)}) %collective-permute-start.7) | collective-permute-done | bytes 196640 | tf_op jit(solution)/shard_map/ppermute | solution.py:376
  224.2 7.9 collective-permute-done.8.p2
  247.2 18.4 %collective-permute-done.11 = bf16[256,1536]{1,0:T(8,128)(2,1)S(1)} collective-permute-done((bf16[256,1536]{1,0:T(8,128)(2,1)S(1)}, bf16[256,1536]{1,0:T(8,128)(2,1)S(1)}, u32[]{:S(2)}, u32[]{:S(2)}) %collective-permute-start.11) | collective-permute-done | bytes 786464 | tf_op jit(solution)/shard_map/ppermute | solution.py:359
  268.7 13.7 %collective-permute-done.18 = bf16[256,1536]{1,0:T(8,128)(2,1)S(1)} collective-permute-done((bf16[256,1536]{1,0:T(8,128)(2,1)S(1)}, bf16[256,1536]{1,0:T(8,128)(2,1)S(1)}, u32[]{:S(2)}, u32[]{:S(2)}) %collective-permute-start.18) | collective-permute-done | bytes 786464 | tf_op jit(solution)/shard_map/ppermute | solution.py:359
  285.7 12.8 %collective-permute-done.13 = bf16[256,1536]{1,0:T(8,128)(2,1)} collective-permute-done((bf16[256,1536]{1,0:T(8,128)(2,1)S(1)}, bf16[256,1536]{1,0:T(8,128)(2,1)}, u32[]{:S(2)}, u32[]{:S(2)}) %collective-permute-start.13) | collective-permute-done | bytes 786464 | tf_op jit(solution)/shard_map/ppermute | solution.py:359
  299.5 11.3 %copy.155 = bf16[2,4,3,768,256]{4,1,3,0,2:T(4,128)(2,1)S(1)} copy(bf16[2,4,3,768,256]{4,3,2,1,0:T(8,128)(2,1)} %bitcast.176) | data formatting | bytes 18874368 | tf_op jit(solution)/shard_map/reshape | solution.py:437
  328.3 7.2 multiply_convert_fusion
  353.1 15.4 %collective-permute-done.21 = bf16[256,1536]{1,0:T(8,128)(2,1)S(1)} collective-permute-done((bf16[256,1536]{1,0:T(8,128)(2,1)S(1)}, bf16[256,1536]{1,0:T(8,128)(2,1)S(1)}, u32[]{:S(2)}, u32[]{:S(2)}) %collective-permute-start.21) | collective-permute-done | bytes 786464 | tf_op jit(solution)/shard_map/ppermute | solution.py:359
  368.6 16.4 %collective-permute-done.16 = bf16[256,1536]{1,0:T(8,128)(2,1)S(1)} collective-permute-done((bf16[256,1536]{1,0:T(8,128)(2,1)S(1)}, bf16[256,1536]{1,0:T(8,128)(2,1)S(1)}, u32[]{:S(2)}, u32[]{:S(2)}) %collective-permute-start.16) | collective-permute-done | bytes 786464 | tf_op jit(solution)/shard_map/ppermute | solution.py:359
  390.4 17.6 %collective-permute-done.23.g2 = bf16[256,1536]{1,0:T(8,128)(2,1)S(1)} collective-permute-done((bf16[256,1536]{1,0:T(8,128)(2,1)S(1)}, bf16[256,1536]{1,0:T(8,128)(2,1)S(1)}, u32[]{:S(2)}, u32[]{:S(2)}) %collective-permute-start.23) | collective-permute-done | bytes 786464 | tf_op jit(solution)/shard_map/ppermute | solution.py:359
  411.1 6.5 out_back.1
  417.6 17.8 %collective-permute-start.25 = (bf16[256,384]{1,0:T(8,128)(2,1)}, bf16[256,384]{1,0:T(8,128)(2,1)S(1)}, u32[]{:S(2)}, u32[]{:S(2)}) collective-permute-start(bf16[256,384]{1,0:T(8,128)(2,1)} %get-tuple-element.63), channel_id=1, source_target_pairs={{0,1},{1,0},{2,3},{3,2},{4,5},{5,4},{6,7},{7,6},{8,9},{9,8},{10,11... | collective-permute-start | bytes 589832 | tf_op jit(solution)/shard_map/ppermute | solution.py:376
  443.0 9.8 %collective-permute-done.26.g2 = bf16[256,384]{1,0:T(8,128)(2,1)S(1)} collective-permute-done((bf16[256,384]{1,0:T(8,128)(2,1)}, bf16[256,384]{1,0:T(8,128)(2,1)S(1)}, u32[]{:S(2)}, u32[]{:S(2)}) %collective-permute-start.26) | collective-permute-done | bytes 196640 | tf_op jit(solution)/shard_map/ppermute | solution.py:376
  453.5 38.9 %attend_back.1 = (bf16[256,384]{1,0:T(8,128)(2,1)}, bf16[256,384]{1,0:T(8,128)(2,1)}, bf16[256,384]{1,0:T(8,128)(2,1)}, bf16[256,384]{1,0:T(8,128)(2,1)}, bf16[4...) custom-call(s32[2]{0:T(128)} %pad_add_fusion.ids, bf16[4096,128]{1,0:T(8,128)(2,1)} %get-tuple-element.56.q_s, ...), custom_call_target="tpu_custom_call" | custom-call | flops 22000001024 | bytes 12000000 | tf_op jit(solution)/shard_map/attend_back/pallas_call | solution.py:194
  509.3 6.6 collective-permute-done.29.q2
  518.1 14.7 %collective-permute-done.33.k2 = bf16[256,384]{1,0:T(8,128)(2,1)S(1)} collective-permute-done((bf16[256,384]{1,0:T(8,128)(2,1)}, bf16[256,384]{1,0:T(8,128)(2,1)S(1)}, u32[]{:S(2)}, u32[]{:S(2)}) %collective-permute-start.33) | collective-permute-done | bytes 196640 | tf_op jit(solution)/shard_map/ppermute | solution.py:376
  533.5 10.3 %project_back.1 = (bf16[2,256,1536]{2,1,0:T(8,128)(2,1)}, bf16[2,256,1536]{2,1,0:T(8,128)(2,1)}, bf16[4,192,1536]{2,1,0:T(8,128)(2,1)}) custom-call(s32[2]{0:T(128)} %pad_add_fusion.ids, bf16[256,384]{1,0:T(8,128)(2,1)} %get-tuple-element.66.q0, bf16[256,384]{1,0:T(8,128)(2,1)} %copy-done.40, bf16[256,384]{1,0:T(8,128)(2,1)} %copy-done.42, ...), custom_call_target="tpu_custom_call" | custom-call | flops 5000000000 | bytes 14000000 | tf_op jit(solution)/shard_map/project_back/pallas_call | solution.py:346
  561.1 6.7 convolution_convert_fusion.1
  578.2 6.9 convolution_convert_fusion
  608.3 51.7 %psum.23 = f32[3]{0:T(128)S(1)} all-reduce(f32[3]{0:T(128)S(1)} %pad_maximum_fusion.6), channel_id=1, replica_groups=mesh['y'=2,'x'=2,'c'=2,'z'=4] {'y','x','c','z'}, use_global_device_ids=true, to_apply=%region_16.17 | all-reduce | flops 3 | bytes 24 | tf_op jit(solution)/shard_map/psum | solution.py:521
  680.3 115.0 %reduce-scatter.5.cloned.1.call-done = bf16[1,3,768,256]{3,2,1,0:T(8,128)(2,1)} async-done(((bf16[8,3,768,256]{3,2,1,0:T(8,128)(2,1)}), bf16[1,3,768,256]{3,2,1,0:T(8,128)(2,1)}) %reduce-scatter.5.cloned.1.call-update) | async-done | bytes 1179664 | tf_op jit(solution)/shard_map/reduce_scatter | solution.py:477
  805.0 12.3 %all-to-all-done.3 = bf16[4,3,192,256]{3,2,1,0:T(8,128)(2,1)S(1)} async-done(((bf16[4,3,192,256]{3,2,1,0:T(8,128)(2,1)}), bf16[4,3,192,256]{3,2,1,0:T(8,128)(2,1)S(1)}, u32[]{:S(2)}, u32[]{:S(2)}) %all-to-all-start.3) | async-done | bytes 1179680 | tf_op jit(solution)/shard_map/all_to_all | solution.py:391
  822.0 10.1 %all-reduce = (f32[192]{0:T(256)}, f32[192]{0:T(256)}) all-reduce(f32[192]{0:T(256)S(1)} %add_add_fusion, f32[192]{0:T(256)S(1)} %add.126), channel_id=1, replica_groups=mesh['y'=2,'x'=2,'c'=2,'z'=4] {'z'}, use_global_device_ids=true, to_apply=%region_9.10 | all-reduce | flops 384 | bytes 3072 | tf_op jit(solution)/shard_map/psum | solution.py:518
  (299 shorter events, 212.2 us)
Async XLA Ops:
  7.2 88.0 %all-gather.3.cloned.1.call-start = ((), (), s32[]{:S(2)}) async-start(), calls=%async_computation.6 | async-start | bytes 3981312 | tf_op jit(solution)/shard_map/all_gather | solution.py:419
  29.5 270.0 %all-gather.5.cloned.1.call-start = ((), (), s32[]{:S(2)}) async-start(), calls=%async_computation.7 | async-start | bytes 10616832 | tf_op jit(solution)/shard_map/all_gather | solution.py:436
  51.8 610.8 %reduce-scatter.3.cloned.1.call-start = ((), (), s32[]{:S(2)}) async-start(), calls=%async_computation.8 | async-start | bytes 3981312 | tf_op jit(solution)/shard_map/reduce_scatter | solution.py:505
  53.4 19.3 %collective-permute-start.1 = (bf16[256,1536]{1,0:T(8,128)(2,1)S(1)}, bf16[256,1536]{1,0:T(8,128)(2,1)S(1)}, u32[]{:S(2)}, u32[]{:S(2)}) collective-permute-start(bf16[256,1536]{1,0:T(8,128)(2,1)S(1)} %fusion.3.x0), channel_id=1, source_target_pairs={{0,8},{8,0},{1,9},{9,1},{2,10},{10,2},{3,11},{11,3},{4,12},{12,4},... | collective-permute-start | bytes 2359304 | tf_op jit(solution)/shard_map/ppermute | solution.py:359
  53.7 45.6 %collective-permute-start = (bf16[256,1536]{1,0:T(8,128)(2,1)S(1)}, bf16[256,1536]{1,0:T(8,128)(2,1)S(1)}, u32[]{:S(2)}, u32[]{:S(2)}) collective-permute-start(bf16[256,1536]{1,0:T(8,128)(2,1)S(1)} %fusion.3.x0), channel_id=1, source_target_pairs={{0,4},{4,0},{1,5},{5,1},{2,6},{6,2},{3,7},{7,3},{8,12},{12,8},{9,1... | collective-permute-start | bytes 2359304 | tf_op jit(solution)/shard_map/ppermute | solution.py:359
  72.7 26.6 %collective-permute-start.2 = (bf16[256,1536]{1,0:T(8,128)(2,1)S(1)}, bf16[256,1536]{1,0:T(8,128)(2,1)}, u32[]{:S(2)}, u32[]{:S(2)}) collective-permute-start(bf16[256,1536]{1,0:T(8,128)(2,1)S(1)} %collective-permute-done.1.x2), channel_id=1, source_target_pairs={{0,4},{4,0},{1,5},{5,1},{2,6},{6,2},{3,7},{7,3},{8,12},{12,8},{9,1... | collective-permute-start | bytes 2359304 | tf_op jit(solution)/shard_map/ppermute | solution.py:359
  111.1 22.4 %collective-permute-start.5 = (bf16[256,768]{1,0:T(8,128)(2,1)}, bf16[256,768]{1,0:T(8,128)(2,1)S(1)}, u32[]{:S(2)}, u32[]{:S(2)}) collective-permute-start(bf16[256,768]{1,0:T(8,128)(2,1)} %get-tuple-element.49), channel_id=1, source_target_pairs={{0,3},{1,2},{2,1},{3,0},{4,7},{5,6},{6,5},{7,4},{8,11},{9,10},{10,... | collective-permute-start | bytes 1179656 | tf_op jit(solution)/shard_map/ppermute | solution.py:376
  112.2 68.3 %collective-permute-start.4 = (bf16[256,768]{1,0:T(8,128)(2,1)}, bf16[256,768]{1,0:T(8,128)(2,1)S(1)}, u32[]{:S(2)}, u32[]{:S(2)}) collective-permute-start(bf16[256,768]{1,0:T(8,128)(2,1)} %get-tuple-element.48), channel_id=1, source_target_pairs={{0,2},{1,3},{2,0},{3,1},{4,6},{5,7},{6,4},{7,5},{8,10},{9,11},{10,... | collective-permute-start | bytes 1179656 | tf_op jit(solution)/shard_map/ppermute | solution.py:376
  113.5 67.0 %collective-permute-start.3 = (bf16[256,768]{1,0:T(8,128)(2,1)}, bf16[256,768]{1,0:T(8,128)(2,1)S(1)}, u32[]{:S(2)}, u32[]{:S(2)}) collective-permute-start(bf16[256,768]{1,0:T(8,128)(2,1)} %get-tuple-element.47), channel_id=1, source_target_pairs={{0,1},{1,0},{2,3},{3,2},{4,5},{5,4},{6,7},{7,6},{8,9},{9,8},{10,11... | collective-permute-start | bytes 1179656 | tf_op jit(solution)/shard_map/ppermute | solution.py:376
  205.8 18.4 %collective-permute-start.7 = (bf16[256,384]{1,0:T(8,128)(2,1)}, bf16[256,384]{1,0:T(8,128)(2,1)S(1)}, u32[]{:S(2)}, u32[]{:S(2)}) collective-permute-start(bf16[256,384]{1,0:T(8,128)(2,1)} %get-tuple-element.51), channel_id=1, source_target_pairs={{0,1},{1,0},{2,3},{3,2},{4,5},{5,4},{6,7},{7,6},{8,9},{9,8},{10,11... | collective-permute-start | bytes 589832 | tf_op jit(solution)/shard_map/ppermute | solution.py:376
  205.9 26.3 %collective-permute-start.8 = (bf16[256,384]{1,0:T(8,128)(2,1)}, bf16[256,384]{1,0:T(8,128)(2,1)S(1)}, u32[]{:S(2)}, u32[]{:S(2)}) collective-permute-start(bf16[256,384]{1,0:T(8,128)(2,1)} %get-tuple-element.52), channel_id=1, source_target_pairs={{0,2},{1,3},{2,0},{3,1},{4,6},{5,7},{6,4},{7,5},{8,10},{9,11},{10,... | collective-permute-start | bytes 589832 | tf_op jit(solution)/shard_map/ppermute | solution.py:376
  206.6 26.4 %collective-permute-start.9 = (bf16[256,384]{1,0:T(8,128)(2,1)}, bf16[256,384]{1,0:T(8,128)(2,1)S(1)}, u32[]{:S(2)}, u32[]{:S(2)}) collective-permute-start(bf16[256,384]{1,0:T(8,128)(2,1)} %get-tuple-element.53), channel_id=1, source_target_pairs={{0,3},{1,2},{2,1},{3,0},{4,7},{5,6},{6,5},{7,4},{8,11},{9,10},{10,... | collective-permute-start | bytes 589832 | tf_op jit(solution)/shard_map/ppermute | solution.py:376
  245.1 20.4 %collective-permute-start.11 = (bf16[256,1536]{1,0:T(8,128)(2,1)S(1)}, bf16[256,1536]{1,0:T(8,128)(2,1)S(1)}, u32[]{:S(2)}, u32[]{:S(2)}) collective-permute-start(bf16[256,1536]{1,0:T(8,128)(2,1)S(1)} %fusion.18), channel_id=1, source_target_pairs={{0,8},{8,0},{1,9},{9,1},{2,10},{10,2},{3,11},{11,3},{4,12},{12,4},... | collective-permute-start | bytes 2359304 | tf_op jit(solution)/shard_map/ppermute | solution.py:359
  246.7 35.7 %collective-permute-start.18 = (bf16[256,1536]{1,0:T(8,128)(2,1)S(1)}, bf16[256,1536]{1,0:T(8,128)(2,1)S(1)}, u32[]{:S(2)}, u32[]{:S(2)}) collective-permute-start(bf16[256,1536]{1,0:T(8,128)(2,1)S(1)} %copy-done.5), channel_id=1, source_target_pairs={{0,8},{8,0},{1,9},{9,1},{2,10},{10,2},{3,11},{11,3},{4,12},{12,4},... | collective-permute-start | bytes 2359304 | tf_op jit(solution)/shard_map/ppermute | solution.py:359
  247.2 36.2 %collective-permute-start.17 = (bf16[256,1536]{1,0:T(8,128)(2,1)S(1)}, bf16[256,1536]{1,0:T(8,128)(2,1)S(1)}, u32[]{:S(2)}, u32[]{:S(2)}) collective-permute-start(bf16[256,1536]{1,0:T(8,128)(2,1)S(1)} %copy-done.5), channel_id=1, source_target_pairs={{0,4},{4,0},{1,5},{5,1},{2,6},{6,2},{3,7},{7,3},{8,12},{12,8},{9,1... | collective-permute-start | bytes 2359304 | tf_op jit(solution)/shard_map/ppermute | solution.py:359
  267.0 31.5 %collective-permute-start.13 = (bf16[256,1536]{1,0:T(8,128)(2,1)S(1)}, bf16[256,1536]{1,0:T(8,128)(2,1)}, u32[]{:S(2)}, u32[]{:S(2)}) collective-permute-start(bf16[256,1536]{1,0:T(8,128)(2,1)S(1)} %multiply_convert_fusion.3), channel_id=1, source_target_pairs={{0,8},{8,0},{1,9},{9,1},{2,10},{10,2},{3,11},{11,3},{4,12},{12,4},... | collective-permute-start | bytes 2359304 | tf_op jit(solution)/shard_map/ppermute | solution.py:359
  285.2 31.1 %collective-permute-start.12 = (bf16[256,1536]{1,0:T(8,128)(2,1)S(1)}, bf16[256,1536]{1,0:T(8,128)(2,1)}, u32[]{:S(2)}, u32[]{:S(2)}) collective-permute-start(bf16[256,1536]{1,0:T(8,128)(2,1)S(1)} %multiply_convert_fusion.3), channel_id=1, source_target_pairs={{0,4},{4,0},{1,5},{5,1},{2,6},{6,2},{3,7},{7,3},{8,12},{12,8},{9,1... | collective-permute-start | bytes 2359304 | tf_op jit(solution)/shard_map/ppermute | solution.py:359
  298.5 17.8 %collective-permute-start.14 = (bf16[256,1536]{1,0:T(8,128)(2,1)}, bf16[256,1536]{1,0:T(8,128)(2,1)}, u32[]{:S(2)}, u32[]{:S(2)}) collective-permute-start(bf16[256,1536]{1,0:T(8,128)(2,1)} %collective-permute-done.13), channel_id=1, source_target_pairs={{0,4},{4,0},{1,5},{5,1},{2,6},{6,2},{3,7},{7,3},{8,12},{12,8},{9,1... | collective-permute-start | bytes 2359304 | tf_op jit(solution)/shard_map/ppermute | solution.py:359
  348.2 20.4 %collective-permute-start.21 = (bf16[256,1536]{1,0:T(8,128)(2,1)S(1)}, bf16[256,1536]{1,0:T(8,128)(2,1)S(1)}, u32[]{:S(2)}, u32[]{:S(2)}) collective-permute-start(bf16[256,1536]{1,0:T(8,128)(2,1)S(1)} %fusion.20), channel_id=1, source_target_pairs={{0,8},{8,0},{1,9},{9,1},{2,10},{10,2},{3,11},{11,3},{4,12},{12,4},... | collective-permute-start | bytes 2359304 | tf_op jit(solution)/shard_map/ppermute | solution.py:359
  351.5 33.5 %collective-permute-start.16 = (bf16[256,1536]{1,0:T(8,128)(2,1)S(1)}, bf16[256,1536]{1,0:T(8,128)(2,1)S(1)}, u32[]{:S(2)}, u32[]{:S(2)}) collective-permute-start(bf16[256,1536]{1,0:T(8,128)(2,1)S(1)} %fusion.19), channel_id=1, source_target_pairs={{0,8},{8,0},{1,9},{9,1},{2,10},{10,2},{3,11},{11,3},{4,12},{12,4},... | collective-permute-start | bytes 2359304 | tf_op jit(solution)/shard_map/ppermute | solution.py:359
  388.8 19.1 %collective-permute-start.23 = (bf16[256,1536]{1,0:T(8,128)(2,1)S(1)}, bf16[256,1536]{1,0:T(8,128)(2,1)S(1)}, u32[]{:S(2)}, u32[]{:S(2)}) collective-permute-start(bf16[256,1536]{1,0:T(8,128)(2,1)S(1)} %get-tuple-element.109.g0), channel_id=1, source_target_pairs={{0,8},{8,0},{1,9},{9,1},{2,10},{10,2},{3,11},{11,3},{4,12},{12,4},... | collective-permute-start | bytes 2359304 | tf_op jit(solution)/shard_map/ppermute | solution.py:359
  390.3 17.6 %collective-permute-start.22 = (bf16[256,1536]{1,0:T(8,128)(2,1)S(1)}, bf16[256,1536]{1,0:T(8,128)(2,1)S(1)}, u32[]{:S(2)}, u32[]{:S(2)}) collective-permute-start(bf16[256,1536]{1,0:T(8,128)(2,1)S(1)} %get-tuple-element.109.g0), channel_id=1, source_target_pairs={{0,4},{4,0},{1,5},{5,1},{2,6},{6,2},{3,7},{7,3},{8,12},{12,8},{9,1... | collective-permute-start | bytes 2359304 | tf_op jit(solution)/shard_map/ppermute | solution.py:359
  417.6 25.3 %collective-permute-start.25 = (bf16[256,384]{1,0:T(8,128)(2,1)}, bf16[256,384]{1,0:T(8,128)(2,1)S(1)}, u32[]{:S(2)}, u32[]{:S(2)}) collective-permute-start(bf16[256,384]{1,0:T(8,128)(2,1)} %get-tuple-element.63), channel_id=1, source_target_pairs={{0,1},{1,0},{2,3},{3,2},{4,5},{5,4},{6,7},{7,6},{8,9},{9,8},{10,11... | collective-permute-start | bytes 589832 | tf_op jit(solution)/shard_map/ppermute | solution.py:376
  435.4 17.3 %collective-permute-start.26 = (bf16[256,384]{1,0:T(8,128)(2,1)}, bf16[256,384]{1,0:T(8,128)(2,1)S(1)}, u32[]{:S(2)}, u32[]{:S(2)}) collective-permute-start(bf16[256,384]{1,0:T(8,128)(2,1)} %get-tuple-element.64), channel_id=1, source_target_pairs={{0,2},{1,3},{2,0},{3,1},{4,6},{5,7},{6,4},{7,5},{8,10},{9,11},{10,... | collective-permute-start | bytes 589832 | tf_op jit(solution)/shard_map/ppermute | solution.py:376
  435.4 17.3 %collective-permute-start.27 = (bf16[256,384]{1,0:T(8,128)(2,1)}, bf16[256,384]{1,0:T(8,128)(2,1)S(1)}, u32[]{:S(2)}, u32[]{:S(2)}) collective-permute-start(bf16[256,384]{1,0:T(8,128)(2,1)} %get-tuple-element.65), channel_id=1, source_target_pairs={{0,3},{1,2},{2,1},{3,0},{4,7},{5,6},{6,5},{7,4},{8,11},{9,10},{10,... | collective-permute-start | bytes 589832 | tf_op jit(solution)/shard_map/ppermute | solution.py:376
  498.8 17.2 %collective-permute-start.29 = (bf16[256,384]{1,0:T(8,128)(2,1)S(1)}, bf16[256,384]{1,0:T(8,128)(2,1)S(1)}, u32[]{:S(2)}, u32[]{:S(2)}) collective-permute-start(bf16[256,384]{1,0:T(8,128)(2,1)S(1)} %copy-done.43), channel_id=1, source_target_pairs={{0,2},{1,3},{2,0},{3,1},{4,6},{5,7},{6,4},{7,5},{8,10},{9,11},{10,... | collective-permute-start | bytes 589832 | tf_op jit(solution)/shard_map/ppermute | solution.py:376
  498.8 17.2 %collective-permute-start.30 = (bf16[256,384]{1,0:T(8,128)(2,1)S(1)}, bf16[256,384]{1,0:T(8,128)(2,1)S(1)}, u32[]{:S(2)}, u32[]{:S(2)}) collective-permute-start(bf16[256,384]{1,0:T(8,128)(2,1)S(1)} %copy-done.41), channel_id=1, source_target_pairs={{0,3},{1,2},{2,1},{3,0},{4,7},{5,6},{6,5},{7,4},{8,11},{9,10},{10,... | collective-permute-start | bytes 589832 | tf_op jit(solution)/shard_map/ppermute | solution.py:376
  506.0 26.8 %collective-permute-start.33 = (bf16[256,384]{1,0:T(8,128)(2,1)}, bf16[256,384]{1,0:T(8,128)(2,1)S(1)}, u32[]{:S(2)}, u32[]{:S(2)}) collective-permute-start(bf16[256,384]{1,0:T(8,128)(2,1)} %get-tuple-element.74), channel_id=1, source_target_pairs={{0,2},{1,3},{2,0},{3,1},{4,6},{5,7},{6,4},{7,5},{8,10},{9,11},{10,... | collective-permute-start | bytes 589832 | tf_op jit(solution)/shard_map/ppermute | solution.py:376
  506.9 25.9 %collective-permute-start.34 = (bf16[256,384]{1,0:T(8,128)(2,1)}, bf16[256,384]{1,0:T(8,128)(2,1)S(1)}, u32[]{:S(2)}, u32[]{:S(2)}) collective-permute-start(bf16[256,384]{1,0:T(8,128)(2,1)} %get-tuple-element.75), channel_id=1, source_target_pairs={{0,3},{1,2},{2,1},{3,0},{4,7},{5,6},{6,5},{7,4},{8,11},{9,10},{10,... | collective-permute-start | bytes 589832 | tf_op jit(solution)/shard_map/ppermute | solution.py:376
  547.9 247.4 %reduce-scatter.5.cloned.1.call-start = ((), (), s32[]{:S(2)}) async-start(), calls=%async_computation.9 | async-start | bytes 10616832 | tf_op jit(solution)/shard_map/reduce_scatter | solution.py:477
  605.1 55.4 %collective-permute-start.36 = (bf16[256,1536]{1,0:T(8,128)(2,1)}, bf16[256,1536]{1,0:T(8,128)(2,1)S(1)}, u32[]{:S(2)}, u32[]{:S(2)}) collective-permute-start(bf16[256,1536]{1,0:T(8,128)(2,1)} %fusion.21), channel_id=1, source_target_pairs={{0,8},{8,0},{1,9},{9,1},{2,10},{10,2},{3,11},{11,3},{4,12},{12,4},... | collective-permute-start | bytes 2359304 | tf_op jit(solution)/shard_map/ppermute | solution.py:359
  797.7 19.7 %all-to-all-start.3 = ((bf16[4,3,192,256]{3,2,1,0:T(8,128)(2,1)}), bf16[4,3,192,256]{3,2,1,0:T(8,128)(2,1)S(1)}, u32[]{:S(2)}, u32[]{:S(2)}) async-start(bf16[4,3,192,256]{3,2,1,0:T(8,128)(2,1)} %copy.136), calls=%async_computation.5 | async-start | bytes 2359296 | tf_op jit(solution)/shard_map/all_to_all | solution.py:391
  (72 other events, 1032.7 us)
Sparse Core Ops, SparseCore 0:
  29.6 65.5 all-gather.2
  97.2 183.8 all-gather.4
  548.0 80.4 reduce-scatter.2
  632.0 163.2 reduce-scatter.4

commit v2 on v1

v2 whole, which is shorter than its diff:
```python
import functools
import jax
import jax.numpy as jnp
from jax import lax
from jax.experimental import pallas as pl
from jax.experimental.pallas import tpu as pltpu
from jax.sharding import Mesh, PartitionSpec as P

HEAD = 96
LANES = 128
SEQUENCE_LENGTH = 4096
SPANS = 4
EPSILON = 1e-05
ROPE_BASE = 100000.0
MASKED = -1e30
LOG2E = 1.4426950408889634
NT = (((1,), (1,)), ((), ()))
NN = (((1,), (0,)), ((), ()))
TN = (((0,), (0,)), ((), ()))
F32 = jnp.float32
BF16 = jnp.bfloat16
VMEM_LIMIT = 60 * 1024 * 1024


def mm(left, right, dims):
    return lax.dot_general(left, right, dims, preferred_element_type=F32)


def widen(piece):
    return jnp.concatenate([piece, jnp.zeros((piece.shape[0], LANES - HEAD), piece.dtype)], axis=1)


def swapped(value):
    half = HEAD // 2
    return jnp.concatenate([value[:, half:HEAD], value[:, :half]], axis=1)


def attend_kernel(ids, own, other, out, q_s, kv_s, o_s, lse_s, acc_s, vt_s, *, block, tile):
    z, t = ids[0], ids[1]
    c = lax.rem(t, 2)
    spans = 4
    rows_all = q_s.shape[0]
    for zj in range(4):
        for r in range(spans):
            at = pl.multiple_of(((t ^ r) * spans + zj) * block, block)
            at_other = pl.multiple_of(((t ^ 1 ^ r) * spans + zj) * block, block)
            q_s[pl.ds(at, block), :] = widen(own[zj, :, r * HEAD : (r + 1) * HEAD])
            kv_s[c, pl.ds(at, block), :] = widen(own[zj, :, (spans + r) * HEAD : (spans + r + 1) * HEAD])
            kv_s[1 - c, pl.ds(at_other, block), :] = widen(other[zj, :, r * HEAD : (r + 1) * HEAD])
    factor = HEAD ** (-0.5) * LOG2E
    is_count = lax.broadcasted_iota(jnp.int32, (tile, LANES), 1) == HEAD

    def values(i, _):
        rows = pl.ds(pl.multiple_of(i * tile, tile), tile)
        vals = kv_s[1, rows, :]
        vt_s[:, rows] = jnp.transpose(jnp.where(is_count, jnp.ones_like(vals), vals))
        return 0

    lax.fori_loop(0, rows_all // tile, values, 0)

    def step(query, j, before, mask):
        rows = pl.ds(pl.multiple_of(j * tile, tile), tile)
        scores = mm(kv_s[0, rows, :], query, NT) * factor
        if mask is not None:
            scores = jnp.where(mask, scores, MASKED)
        top = jnp.maximum(before, jnp.max(scores, axis=0, keepdims=True))
        expo = jnp.exp2(scores - top).astype(BF16)
        acc_s[...] = acc_s[...] * jnp.exp2(before - top) + mm(vt_s[:, rows], expo, NN)
        return top

    def row_block(i, _):
        at = pl.multiple_of(i * tile, tile)
        query = q_s[pl.ds(at, tile), :]
        acc_s[...] = jnp.zeros_like(acc_s)
        top = lax.fori_loop(0, i, lambda j, top: step(query, j, top, None), jnp.full((1, tile), MASKED, F32))
        mask = lax.broadcasted_iota(jnp.int32, (tile, tile), 0) <= lax.broadcasted_iota(jnp.int32, (tile, tile), 1)
        top = step(query, i, top, mask)
        acc = acc_s[...]
        denom = acc[HEAD : HEAD + 1, :]
        o_s[pl.ds(at, tile), :] = jnp.transpose(acc / denom).astype(BF16)
        lse_s[:, pl.ds(at, tile)] = jnp.broadcast_to(top + jnp.log2(denom), (8, tile))
        return 0

    lax.fori_loop(0, rows_all // tile, row_block, 0)
    for zj in range(4):
        for r in range(spans):
            at = pl.multiple_of(((t ^ r) * spans + zj) * block, block)
            out[zj, :, r * HEAD : (r + 1) * HEAD] = o_s[pl.ds(at, block), :HEAD]


VM = pl.BlockSpec(memory_space=pltpu.VMEM)
SM = pl.BlockSpec(memory_space=pltpu.SMEM)


def shape(dims, dtype=BF16):
    return jax.ShapeDtypeStruct(dims, dtype)


def params():
    return pltpu.CompilerParams(vmem_limit_bytes=VMEM_LIMIT)


def attend(ids, own, other, tile=1024):
    block = own.shape[1]
    rows = block * 16
    return pl.pallas_call(
        functools.partial(attend_kernel, block=block, tile=tile),
        out_shape=[shape((4, block, 4 * HEAD)), shape((rows, LANES)), shape((2, rows, LANES)), shape((rows, LANES)), shape((8, rows), F32)],
        in_specs=[SM] + [VM] * 2,
        out_specs=[VM] * 5,
        scratch_shapes=[pltpu.VMEM((LANES, tile), F32), pltpu.VMEM((LANES, rows), BF16)],
        compiler_params=params(),
        cost_estimate=pl.CostEstimate(flops=int(21e9), bytes_accessed=1, transcendentals=0),
        name="attend",
    )(ids, own, other)


def attend_back_kernel(ids, q_s, kv_s, o_s, lse_s, cos_s, sin_s, g, dq_out, keep_out, give_out, g_s, qx_s, kx_s, delta_s, dq_s, dk_s, dv_s, *, block, tile):
    z, t = ids[0], ids[1]
    spans = 4
    rows_all = q_s.shape[0]
    tiles = rows_all // tile
    for zj in range(4):
        for r in range(spans):
            at = pl.multiple_of(((t ^ r) * spans + zj) * block, block)
            g_s[pl.ds(at, block), :] = widen(g[zj, :, r * HEAD : (r + 1) * HEAD])

    def prepare(i, _):
        at = pl.multiple_of(i * tile, tile)
        rows = pl.ds(at, tile)
        query = q_s[rows, :]
        keys = kv_s[0, rows, :]
        qx_s[rows, :LANES] = query
        qx_s[rows, LANES:] = widen(swapped(query))
        kx_s[rows, :LANES] = keys
        kx_s[rows, LANES:] = widen(swapped(keys))
        both = g_s[rows, :].astype(F32) * o_s[rows, :].astype(F32)
        delta = jnp.sum(both, axis=1, keepdims=True)
        delta_s[:, rows] = jnp.transpose(jnp.broadcast_to(delta, (tile, LANES)))[:8]
        dq_s[rows, :] = jnp.zeros((tile, 2 * LANES), F32)
        return 0

    lax.fori_loop(0, tiles, prepare, 0)
    factor = HEAD ** (-0.5) * LOG2E
    scale = HEAD ** (-0.5)

    def step(i, keys, vals, kx, mask):
        rows = pl.ds(pl.multiple_of(i * tile, tile), tile)
        query = qx_s[rows, :]
        grad = g_s[rows, :]
        scores = mm(keys, query[:, :LANES], NT) * factor - lse_s[:1, rows]
        if mask is not None:
            scores = jnp.where(mask, scores, MASKED)
        prob = jnp.exp2(scores)
        through = mm(vals, grad, NT)
        ds = (prob * (through - delta_s[:1, rows])).astype(BF16)
        dv_s[...] += mm(prob.astype(BF16), grad, NN)
        dk_s[...] += mm(ds, query, NN)
        dq_s[rows, :] += mm(ds, kx, TN)

    def column_block(j, _):
        rows = pl.ds(pl.multiple_of(j * tile, tile), tile)
        kx = kx_s[rows, :]
        keys = kx[:, :LANES]
        vals = kv_s[1, rows, :]
        dk_s[...] = jnp.zeros_like(dk_s)
        dv_s[...] = jnp.zeros_like(dv_s)
        mask = lax.broadcasted_iota(jnp.int32, (tile, tile), 0) <= lax.broadcasted_iota(jnp.int32, (tile, tile), 1)
        step(j, keys, vals, kx, mask)
        lax.fori_loop(j + 1, tiles, lambda i, _: (step(i, keys, vals, kx, None), 0)[1], 0)
        dk = dk_s[...] * scale
        dk = dk[:, :LANES] * cos_s[rows, :] - dk[:, LANES:] * sin_s[rows, :]
        dv = dv_s[...]
        first = lax.rem(t, 2) == 0
        keep_out[rows, :] = jnp.where(first, dk, dv).astype(BF16)
        give_out[rows, :] = jnp.where(first, dv, dk).astype(BF16)
        return 0

    lax.fori_loop(0, tiles, column_block, 0)
    for zj in range(4):
        for r in range(spans):
            rows = pl.ds(pl.multiple_of(((t ^ r) * spans + zj) * block, block), block)
            dq = dq_s[rows, :] * scale
            dq_out[zj, :, r * HEAD : (r + 1) * HEAD] = (
                dq[:, :LANES] * cos_s[rows, :] - dq[:, LANES:] * sin_s[rows, :]
            ).astype(BF16)[:, :HEAD]


def attend_back(ids, q, kv, o, lse, cosine, sine, grads, tile=1024):
    block = grads.shape[1]
    rows = block * 16
    return pl.pallas_call(
        functools.partial(attend_back_kernel, block=block, tile=tile),
        out_shape=[shape((4, block, 4 * HEAD))] + [shape((rows, LANES))] * 2,
        in_specs=[SM] + [VM] * 7,
        out_specs=[VM] * 3,
        scratch_shapes=[
            pltpu.VMEM((rows, LANES), BF16),
            pltpu.VMEM((rows, 2 * LANES), BF16),
            pltpu.VMEM((rows, 2 * LANES), BF16),
            pltpu.VMEM((8, rows), F32),
            pltpu.VMEM((rows, 2 * LANES), F32),
            pltpu.VMEM((tile, 2 * LANES), F32),
            pltpu.VMEM((tile, LANES), F32),
        ],
        compiler_params=params(),
        cost_estimate=pl.CostEstimate(flops=int(39e9), bytes_accessed=1, transcendentals=0),
        name="attend_back",
    )(ids, q, kv, o, lse, cosine, sine, grads)


def offsets(ids, count, part):
    if count == 1:
        return [0]
    return [pl.multiple_of(ids[2] * part, LANES), pl.multiple_of((1 - ids[2]) * part, LANES)]


def call(kernel, outs, name, scratch=(), micros=0):
    def run(ids, *args):
        return pl.pallas_call(
            kernel,
            out_shape=[shape(*o) if isinstance(o[0], tuple) else shape(o) for o in outs],
            in_specs=[SM] + [VM] * len(args),
            out_specs=[VM] * len(outs),
            scratch_shapes=[pltpu.VMEM(*item) for item in scratch],
            compiler_params=params(),
            cost_estimate=pl.CostEstimate(flops=int(micros * 1e9) + 1, bytes_accessed=1, transcendentals=0),
            name=name,
        )(ids, *args)

    return run


def split(refs, *counts):
    refs = list(refs)
    groups = []
    for count in counts:
        groups.append(refs[:count])
        refs = refs[count:]
    return groups


def prepare_attn(ids, w_query, w_key, w_value, w_out, gain):
    shard = w_query.shape[0]

    def kernel(ids, query, key, value, out, gain, *refs):
        pieces, made = split(refs, SPANS, 1)
        made = made[0]
        scale = gain[...]

        def turned(ref, at):
            return jnp.transpose(ref[:, at * HEAD : (at + 1) * HEAD].astype(F32) * scale).astype(BF16)

        for place in range(SPANS):
            made[place, :HEAD] = turned(query, place)
            made[place, HEAD : 2 * HEAD] = turned(value if place % 2 else key, place // 2)
            made[place, 2 * HEAD :] = jnp.transpose(out[:, place * HEAD : (place + 1) * HEAD].astype(F32)).astype(BF16)
        for r in range(SPANS):
            pieces[r][...] = made[ids[1] ^ r]

    scratch = [((SPANS, 3 * HEAD, shard), BF16)]
    return call(kernel, [(3 * HEAD, shard)] * SPANS, "prepare_attn", scratch)(
        ids, w_query, w_key, w_value, w_out.T, gain
    )


def prepare_ffn(ids, w_gate, w_up, w_down, gain):
    shard = w_gate.shape[0]
    units = w_gate.shape[1] // SPANS

    def kernel(ids, gate, up, down, gain, *pieces):
        scale = gain[...]
        for r in range(SPANS):
            at = pl.multiple_of((ids[1] ^ r) * units, LANES)
            pieces[r][0] = (gate[:, pl.ds(at, units)].astype(F32) * scale).astype(BF16)
            pieces[r][1] = (up[:, pl.ds(at, units)].astype(F32) * scale).astype(BF16)
            pieces[r][2] = down[:, pl.ds(at, units)]

    return call(kernel, [(3, shard, units)] * SPANS, "prepare_ffn")(ids, w_gate, w_up, w_down.T, gain)


def distinct(items):
    arrays = list({id(item[0]): item[0] for item in items}.values())
    index = {id(array): i for i, array in enumerate(arrays)}

    def rows_of(refs, item, rows):
        return refs[index[id(item[0])]][(*item[1], rows)]

    return arrays, rows_of


def project(ids, x, weights, cosine, sine):
    block = x[0].shape[0]
    parts = len(weights[0])
    part = weights[0][0][0].shape[-1]
    arrays, rows_of = distinct([item for items in weights for item in items])
    first = slice(0, 2 * HEAD)

    def kernel(ids, *refs):
        xs, ws, (cos_s, sin_s), (out,) = split(refs, SPANS, len(arrays), 2, 1)
        z, t = ids[0], ids[1]
        at = offsets(ids, parts, part)
        is_value = lax.rem(t, 2) == 1
        for r, x in enumerate(xs):
            rows = pl.ds(pl.multiple_of(((t ^ r) * SPANS + z) * block, block), block)
            cosine, sine = cos_s[rows, :HEAD], sin_s[rows, :HEAD]
            cos_kv = jnp.where(is_value, 1.0, cosine)
            sin_kv = jnp.where(is_value, 0.0, sine)
            for k in range(4):
                made = sum(mm(x[:, pl.ds(at[p], part)], rows_of(ws, weights[k][p], first), NT) for p in range(parts))
                query, other = made[:, :HEAD], made[:, HEAD:]
                out[z ^ k, :, r * HEAD : (r + 1) * HEAD] = (query * cosine + swapped(query) * sine).astype(BF16)
                out[z ^ k, :, (SPANS + r) * HEAD : (SPANS + r + 1) * HEAD] = (
                    other * cos_kv + swapped(other) * sin_kv
                ).astype(BF16)

    return call(kernel, [(4, block, 8 * HEAD)], "project")(ids, *x, *arrays, cosine, sine)[0]


def out_project(ids, pieces, weights):
    block = pieces.shape[1]
    parts = len(weights[0])
    part = weights[0][0][0].shape[-1]
    width = parts * part
    arrays, rows_of = distinct([item for items in weights for item in items])

    def kernel(ids, *refs):
        (pieces,), ws, (near, far, att, orel) = split(refs, 1, len(arrays), 4)
        at = offsets(ids, parts, part)
        for j in range(4):
            for r in range(SPANS):
                att[r * block : (r + 1) * block, j * HEAD : (j + 1) * HEAD] = pieces[ids[0] ^ j, :, r * HEAD : (r + 1) * HEAD]
            for p in range(parts):
                orel[j * HEAD : (j + 1) * HEAD, pl.ds(at[p], part)] = rows_of(ws, weights[j][p], slice(2 * HEAD, 3 * HEAD))
        for r in (1, 3, 2, 0):
            made = mm(att[r * block : (r + 1) * block, :], orel[...], NN).astype(BF16)
            (far if r % 2 else near)[r // 2] = made

    outs = [(2, block, width)] * 2 + [(4 * block, 4 * HEAD), (4 * HEAD, width)]
    return call(kernel, outs, "out_project")(ids, pieces, *arrays)


def out_back(ids, grads, att, orel, parts):
    block, width = grads[0].shape
    part = width // parts

    def kernel(ids, *refs):
        gs, (att, orel), (ds,), douts, (g_s,) = split(refs, SPANS, 2, 1, parts, 1)
        at = offsets(ids, parts, part)
        for r, grad in enumerate(gs):
            g_s[r * block : (r + 1) * block, :] = grad[...]
        made = mm(g_s[...], orel[...], NT).astype(BF16)
        for r in range(SPANS):
            for j in range(4):
                ds[ids[0] ^ j, :, r * HEAD : (r + 1) * HEAD] = made[r * block : (r + 1) * block, j * HEAD : (j + 1) * HEAD]
        for p in range(parts):
            total = mm(att[...], g_s[:, pl.ds(at[p], part)], TN)
            for k in range(4):
                douts[p][k] = total[k * HEAD : (k + 1) * HEAD].astype(BF16)

    outs = [(4, block, 4 * HEAD)] + [(4, HEAD, part)] * parts
    made = call(kernel, outs, "out_back", [((4 * block, width), BF16)])(ids, *grads, att, orel)
    return made[0], made[1:]


def pack(ids, queries, mine, theirs):
    _, block, wide = queries.shape

    def kernel(ids, queries, mine, theirs, out):
        t = ids[1]
        for zj in range(4):
            out[zj, :, :wide] = queries[zj]
            for r in range(SPANS):
                rows = pl.ds(pl.multiple_of(((t ^ r) * SPANS + zj) * block, block), block)
                total = (mine[rows, :].astype(F32) + theirs[rows, :].astype(F32)).astype(BF16)
                out[zj, :, wide + r * HEAD : wide + (r + 1) * HEAD] = total[:, :HEAD]

    return call(kernel, [(4, block, 2 * wide)], "pack")(ids, queries, mine, theirs)[0]


def project_weights(ids, grads, x, parts):
    block, width = x[0].shape
    part = width // parts

    def kernel(ids, *refs):
        (grads,), xs, (d_out,), das, (x_s,) = split(refs, 1, SPANS, 1, 2 * parts, 1)
        at = offsets(ids, parts, part)
        for j in range(4):
            for r in range(SPANS):
                for half in range(2):
                    lanes = slice((half * SPANS + r) * HEAD, (half * SPANS + r + 1) * HEAD)
                    d_out[r * block : (r + 1) * block, (2 * j + half) * HEAD : (2 * j + half + 1) * HEAD] = grads[
                        ids[0] ^ j, :, lanes
                    ]
        for r, x in enumerate(xs):
            x_s[r * block : (r + 1) * block, :] = x[...]
        for p in reversed(range(parts)):
            total = mm(d_out[...], x_s[:, pl.ds(at[p], part)], TN)
            for k in range(4):
                das[2 * p + (k < 2)][k % 2] = total[2 * k * HEAD : (2 * k + 2) * HEAD].astype(BF16)

    outs = [(4 * block, 8 * HEAD)] + [(2, 2 * HEAD, part)] * (2 * parts)
    made = call(kernel, outs, "project_weights", [((4 * block, width), BF16)])(ids, grads, *x)
    return made[0], made[1:]


def project_tokens(ids, grads, weights):
    rows = grads.shape[0]
    block = rows // SPANS
    parts = len(weights[0])
    part = weights[0][0][0].shape[-1]
    width = parts * part
    arrays, rows_of = distinct([item for items in weights for item in items])

    def kernel(ids, *refs):
        (d_s,), ws, (near, far), (a_s,) = split(refs, 1, len(arrays), 2, 1)
        at = offsets(ids, parts, part)
        for j in range(4):
            for p in range(parts):
                a_s[2 * j * HEAD : (2 * j + 2) * HEAD, pl.ds(at[p], part)] = rows_of(ws, weights[j][p], slice(0, 2 * HEAD))
        for r in (1, 3, 2, 0):
            made = mm(d_s[r * block : (r + 1) * block, :], a_s[...], NN).astype(BF16)
            (far if r % 2 else near)[r // 2] = made

    scratch = [((8 * HEAD, width), BF16)]
    return call(kernel, [(2, block, width)] * 2, "project_tokens", scratch)(ids, grads, *arrays)


def feed(ids, x, grads, weights):
    block, width = x[0].shape
    part, units = weights[0][0].shape[-2:]
    parts = width // part
    rows, every = 2 * block, 4 * units
    arrays = list({id(item[0]): item[0] for item in weights}.values())
    index = {id(array): i for i, array in enumerate(arrays)}

    def kernel(ids, *refs):
        xs, gs, ws, ffn, two, (hid, dgate, dup), (x_s, g_s, w_s) = split(refs, 2, 2, len(arrays), 2, 2, 3, 3)
        at = [pl.multiple_of(place, LANES) for place in offsets(ids, parts, part)]
        for r in range(2):
            x_s[r * block : (r + 1) * block, :] = xs[r][...]
            g_s[r * block : (r + 1) * block, :] = gs[r][...]
        for array, where, m, k, p in weights:
            w_s[m, pl.ds(at[p], part), k * units : (k + 1) * units] = ws[index[id(array)]][where]

        def pair(i, _):
            lanes = pl.ds(pl.multiple_of(i * units, LANES), units)
            gate = mm(x_s[...], w_s[0, :, lanes], NN)
            up = mm(x_s[...], w_s[1, :, lanes], NN)
            back = mm(g_s[...], w_s[2, :, lanes], NN)
            sigma = 1.0 / (1.0 + jnp.exp(-gate))
            swish = gate * sigma
            hid[:, lanes] = (swish * up).astype(BF16)
            dup[:, lanes] = (back * swish).astype(BF16)
            dgate[:, lanes] = (back * up * (sigma * (1.0 + gate * (1.0 - sigma)))).astype(BF16)
            return 0

        lax.fori_loop(0, 4, pair, 0)
        cut = width // 2
        for p in range(2):
            lanes = slice(p * cut, (p + 1) * cut)
            made = mm(dgate[...], w_s[0, lanes], NT) + mm(dup[...], w_s[1, lanes], NT)
            for r in range(2):
                two[r][:, lanes] = made[r * block : (r + 1) * block].astype(BF16)
        for p in range(2):
            lanes = slice(p * cut, (p + 1) * cut)
            made = mm(hid[...], w_s[2, lanes], NT)
            for r in range(2):
                ffn[r][:, lanes] = made[r * block : (r + 1) * block].astype(BF16)

    outs = [(block, width)] * 4 + [(rows, every)] * 3
    scratch = [((rows, width), BF16), ((rows, width), BF16), ((3, width, every), BF16)]
    made = call(kernel, outs, "feed", scratch, 18)(ids, *x, *grads, *arrays)
    return made[:2], made[2:4], made[4:]


def feed_weights(ids, x, grads, near, far, parts):
    block, width = x[0].shape
    part = width // parts
    half, every = near[0].shape
    units = every // 4

    def kernel(ids, *refs):
        xs, gs, ns, fs, outs, (x_s, g_s, h_s) = split(refs, SPANS, SPANS, 3, 3, 4 * parts, 3)
        at = offsets(ids, parts, part)
        for slot, r in enumerate((0, 1, 2, 3)):
            x_s[slot * block : (slot + 1) * block, :] = xs[r][...]
            g_s[slot * block : (slot + 1) * block, :] = gs[r][...]
        for m in range(3):
            h_s[m, :half] = ns[m][...]
            h_s[m, half:] = fs[m][...]
        for p in reversed(range(parts)):
            for m, left in ((2, g_s), (0, x_s), (1, x_s)):
                side = h_s[{0: 1, 1: 2, 2: 0}[m]]
                total = mm(left[:, pl.ds(at[p], part)], side, TN)
                for k in range(4):
                    outs[k * parts + p][m] = total[:, k * units : (k + 1) * units].astype(BF16)

    outs = [(3, part, units)] * (4 * parts)
    scratch = [((4 * block, width), BF16), ((4 * block, width), BF16), ((3, 4 * block, every), BF16)]
    return call(kernel, outs, "feed_weights", scratch, 17)(ids, *x, *grads, *near, *far)


def finish_ffn(ids, pieces, w_gate, w_up, gain):
    _, shard, units = pieces[0].shape
    every = SPANS * units

    def kernel(ids, *refs):
        pieces, (w_gate, w_up, gain), (gate, up, down, sums) = split(refs, SPANS, 3, 4)
        scale = gain[...]
        total = jnp.zeros((shard, 1), F32)
        for r, piece in enumerate(pieces):
            lanes = pl.ds(pl.multiple_of((ids[1] ^ r) * units, LANES), units)
            for m, (out, weight) in enumerate(((gate, w_gate), (up, w_up))):
                grad = piece[m].astype(F32)
                out[:, lanes] = grad * scale
                total += jnp.sum(grad * weight[:, lanes].astype(F32), axis=1, keepdims=True)
            down[:, lanes] = piece[2].astype(F32)
        sums[...] = jnp.transpose(jnp.broadcast_to(total, (shard, LANES)))[:8]

    outs = [((shard, every), F32)] * 3 + [((8, shard), F32)]
    return call(kernel, outs, "finish_ffn")(ids, *pieces, w_gate, w_up, gain)


def finish_attn(ids, pieces, w_query, w_key, w_value, gain):
    shard = pieces[0].shape[1]

    def kernel(ids, *refs):
        pieces, (w_query, w_key, w_value, gain), (query, key, value, out_w, sums), (made,) = split(refs, SPANS, 4, 5, 1)
        scale = gain[...]
        for r, piece in enumerate(pieces):
            made[ids[1] ^ r] = piece[...].astype(F32)
        total = jnp.zeros((shard, 1), F32)
        for place in range(SPANS):
            out_w[:, place * HEAD : (place + 1) * HEAD] = jnp.transpose(made[place, 2 * HEAD :])
            for out, weight, at, rows in (
                (query, w_query, place, 0),
                (value if place % 2 else key, w_value if place % 2 else w_key, place // 2, HEAD),
            ):
                grad = jnp.transpose(made[place, rows : rows + HEAD])
                lanes = slice(at * HEAD, (at + 1) * HEAD)
                out[:, lanes] = grad * scale
                total += jnp.sum(grad * weight[:, lanes].astype(F32), axis=1, keepdims=True)
        sums[...] = jnp.transpose(jnp.broadcast_to(total, (shard, LANES)))[:8]

    outs = [((shard, 4 * HEAD), F32), ((shard, 2 * HEAD), F32), ((shard, 2 * HEAD), F32)]
    outs += [((shard, 4 * HEAD), F32), ((8, shard), F32)]
    scratch = [((SPANS, 3 * HEAD, shard), F32)]
    return call(kernel, outs, "finish_attn", scratch)(ids, *pieces, w_query, w_key, w_value, gain)


def swap(value, axis):
    return lax.ppermute(value, axis, [(0, 1), (1, 0)])


def sent(value, axis, bits):
    return lax.ppermute(value, axis, [(i, i ^ bits) for i in range(lax.axis_size(axis))])


def gather_group(value):
    core = swap(value, "c")
    across = swap(value, "x")
    return value, core, across, swap(across, "c")


def scatter_group(near, far):
    total = near.astype(F32) + swap(far, "c").astype(F32)
    return total[0] + swap(total[1].astype(BF16), "x").astype(F32)


def scatter_halves(near, far):
    far_total = far[0].astype(F32) + swap(far[1], "c").astype(F32)
    crossing = swap(far_total.astype(BF16), "x")
    return near[0].astype(F32) + swap(near[1], "c").astype(F32) + crossing.astype(F32)


def exchange(pieces):
    return lax.all_to_all(pieces, "z", split_axis=0, concat_axis=0, tiled=True)


def spread(pieces):
    return [
        pieces[0],
        swap(pieces[1], "c"),
        swap(pieces[2], "x"),
        lax.ppermute(pieces[3], ("x", "c"), [(i, 3 - i) for i in range(SPANS)]),
    ]


def by_place(pieces, t):
    stacked = jnp.stack(pieces)
    return jnp.stack([lax.dynamic_index_in_dim(stacked, t ^ place, 0, keepdims=False) for place in range(SPANS)])


def beside(mine, dim):
    if lax.axis_size("y") == 2:
        return [mine, swap(mine, "y")]
    return [lax.all_gather(mine, "y", axis=dim, tiled=True)]


def along_z(mine):
    if lax.axis_size("z") != 4:
        return [mine] + [sent(mine, "z", k) for k in range(1, lax.axis_size("z"))]
    far = sent(mine, "z", 3)
    return [mine, sent(mine, "z", 1), sent(far, "z", 1), far]


def onto_z(pieces):
    far = pieces[3].astype(F32) + sent(pieces[2], "z", 1).astype(F32)
    near = pieces[0].astype(F32) + sent(pieces[1], "z", 1).astype(F32)
    return (near + sent(far.astype(BF16), "z", 3).astype(F32)).astype(BF16)


def settled(pieces, parts, dim):
    if parts == 2:
        sums = [
            (pieces[2 * k].astype(F32) + swap(pieces[2 * k + 1], "y").astype(F32)).astype(BF16) for k in range(4)
        ]
    else:
        sums = [lax.psum_scatter(piece, "y", scatter_dimension=dim, tiled=True) for piece in pieces]
    return onto_z(sums)


def over_z(value):
    return value + sum(sent(value, "z", k) for k in range(1, lax.axis_size("z")))


def unit(values):
    scale = lax.rsqrt(jnp.mean(values * values, axis=-1, keepdims=True) + EPSILON)
    return values * scale, scale


def unit_back(values, scale, grad):
    inner = jnp.mean(grad * values, axis=-1, keepdims=True)
    return scale * grad - values * (scale * scale * scale) * inner


def per_device(tokens, w_query, w_key, w_value, w_out, w_gate, w_up, w_down, norm_attn, norm_ffn, grad_out):
    sequences, count = lax.axis_size("y"), lax.axis_size("z")
    parts = 2 if sequences == 2 else 1
    block, width = tokens.shape
    shard = w_query.shape[0]
    t = lax.axis_index("x") * 2 + lax.axis_index("c")
    ids = jnp.stack([lax.axis_index("z"), t, lax.axis_index("y")]).astype(jnp.int32)
    gain_attn = norm_attn.astype(F32)[:, None]
    gain_ffn = norm_ffn.astype(F32)[:, None]

    fence = lax.optimization_barrier

    resid = tokens.astype(F32)
    unit_one, scale_one = unit(resid)
    attn_pieces, low_one = fence((prepare_attn(ids, w_query, w_key, w_value, w_out, gain_attn), unit_one.astype(BF16)))
    attn_mine = by_place(spread(attn_pieces), t).transpose(1, 0, 2).reshape(3 * HEAD, SPANS * shard)
    lane = jnp.arange(LANES)
    freq = ROPE_BASE ** (-(lane % (HEAD // 2) * 2.0) / HEAD)
    inner = jnp.arange(block, dtype=F32)[:, None] * freq
    outer = (jnp.arange(SEQUENCE_LENGTH // block, dtype=F32) * block)[:, None] * freq
    cos_in, sin_in, cos_out, sin_out = jnp.cos(inner), jnp.sin(inner), jnp.cos(outer)[:, None], jnp.sin(outer)[:, None]
    cosine = (cos_out * cos_in - sin_out * sin_in).reshape(SEQUENCE_LENGTH, LANES)
    sine = (sin_out * cos_in + cos_out * sin_in).reshape(SEQUENCE_LENGTH, LANES)
    sine = sine * jnp.where(lane < HEAD // 2, -1.0, 1.0)
    attn_mine, ffn_pieces, cosine, sine, low_one = fence(
        (attn_mine, prepare_ffn(ids, w_gate, w_up, w_down, gain_ffn), cosine, sine, low_one)
    )

    attn_three, attn_one = sent(attn_mine, "z", 3), sent(attn_mine, "z", 1)
    own = beside(attn_mine, 1)
    ffn_mine = by_place(spread(ffn_pieces), t).transpose(1, 0, 2, 3).reshape(3, SPANS * shard, -1)
    core, across = swap(low_one, "c"), swap(low_one, "x")
    ffn_mine, attn_three, attn_one, own = fence((ffn_mine, attn_three, attn_one, own))
    attn_two = sent(attn_three, "z", 1)
    three_one = beside(jnp.stack([attn_three, attn_one]), 2)
    gate_three = sent(ffn_mine[0], "z", 3)
    attn_two, three_one, gate_three, ffn_mine, core, across = fence(
        (attn_two, three_one, gate_three, ffn_mine, core, across)
    )
    x_one = (low_one, core, across, swap(across, "c"))
    two = beside(attn_two, 1)
    attn_weights = [
        [(array, ()) for array in own],
        [(array, (1,)) for array in three_one],
        [(array, ()) for array in two],
        [(array, (0,)) for array in three_one],
    ]
    gate_one, up_three = sent(ffn_mine[0], "z", 1), sent(ffn_mine[1], "z", 3)
    made = project(ids, x_one, attn_weights, cosine, sine)
    made, gate_one, up_three, gate_three, ffn_mine, grad_in = fence(
        (made, gate_one, up_three, gate_three, ffn_mine, grad_out)
    )

    made = exchange(made)
    ffn_own = beside(ffn_mine, 1)
    g_rows = gather_group(grad_in)
    by_one = jnp.stack([ffn_mine[1], gate_three])
    gate_three_one = jnp.stack([gate_three, gate_one])
    made, ffn_own, g_rows, by_one, gate_three_one, down_mine = fence(
        (made, ffn_own, g_rows, by_one, gate_three_one, ffn_mine[2])
    )
    down_three, by_one = sent(down_mine, "z", 3), sent(by_one, "z", 1)
    gate_three_one = beside(gate_three_one, 1)
    other = swap(made[:, :, SPANS * HEAD :], "c")
    attended, q_seq, kv_seq, o_seq, lse = attend(ids, made, other)
    attended, down_three, by_one, gate_three_one, up_three = fence(
        (attended, down_three, by_one, gate_three_one, up_three)
    )
    attended = exchange(attended)
    up_three_one = beside(jnp.stack([up_three, by_one[0]]), 1)
    last_one = jnp.stack([down_mine, up_three, down_three])
    down_three_gate_two = jnp.stack([down_three, by_one[1]])
    attended, up_three_one, last_one, down_three_gate_two = fence(
        (attended, up_three_one, last_one, down_three_gate_two)
    )
    last_one = sent(last_one, "z", 1)
    down_three_gate_two = beside(down_three_gate_two, 1)
    near, far, att, orel = out_project(ids, attended, attn_weights)
    branch_attn = scatter_group(near, far)
    state = resid + branch_attn
    unit_two, scale_two = unit(state)
    low_two, last_one, down_three_gate_two = fence((unit_two.astype(BF16), last_one, down_three_gate_two))
    x_two = gather_group(low_two)
    last_one = beside(last_one, 1)
    x_two, last_one = fence((x_two, last_one))

    ffn_weights = []
    for p in range(parts):
        ffn_weights += [(ffn_own[p], (m,), m, 0, p) for m in range(3)]
        ffn_weights += [(gate_three_one[p], (0,), 0, 3, p), (gate_three_one[p], (1,), 0, 1, p)]
        ffn_weights += [(up_three_one[p], (0,), 1, 3, p), (up_three_one[p], (1,), 1, 1, p)]
        ffn_weights += [(down_three_gate_two[p], (0,), 2, 3, p), (down_three_gate_two[p], (1,), 0, 2, p)]
        ffn_weights += [(last_one[p], (i,), *place, p) for i, place in enumerate(((2, 1), (1, 2), (2, 2)))]
    ffn_far, two_far, kept_far = feed(ids, x_two[2:], g_rows[2:], ffn_weights)
    crossing = (two_far[0].astype(F32) + swap(two_far[1], "c").astype(F32)).astype(BF16)
    crossing, x_near = fence((crossing, x_two[:2]))
    crossing = swap(crossing, "x")
    ffn_near, two_near, kept_near = feed(ids, x_near, g_rows[:2], ffn_weights)
    two_near, crossing = fence((two_near, crossing))
    grad_unit_two = two_near[0].astype(F32) + swap(two_near[1], "c").astype(F32) + crossing.astype(F32)
    grad_state = grad_out.astype(F32) + unit_back(state, scale_two, grad_unit_two)
    state_low, kept_near, ffn_near, ffn_far = fence((grad_state.astype(BF16), kept_near, ffn_near, ffn_far))
    across, core = swap(state_low, "x"), swap(state_low, "c")
    feed_grads = feed_weights(ids, x_two, g_rows, kept_near, kept_far, parts)
    across, core, feed_grads = fence((across, core, feed_grads))
    g_state = (state_low, core, across, swap(across, "c"))

    def home(total):
        pieces = total.reshape(*total.shape[:-2], SPANS, shard, total.shape[-1])
        return spread([lax.dynamic_index_in_dim(pieces, t ^ r, pieces.ndim - 3, keepdims=False) for r in range(SPANS)])

    def home_lanes(total):
        pieces = total.reshape(total.shape[0], SPANS, shard)
        return spread([lax.dynamic_index_in_dim(pieces, t ^ r, 1, keepdims=False) for r in range(SPANS)])

    def crossed(grads, k):
        if parts == 1:
            return lax.psum_scatter(grads[k], "y", scatter_dimension=1, tiled=True)
        return swap(grads[2 * k + 1], "y")

    def added(grads, k, came):
        return came if parts == 1 else (grads[2 * k].astype(F32) + came.astype(F32)).astype(BF16)

    two_came = crossed(feed_grads, 2)
    grad_att, out_grads = out_back(ids, g_state, att, orel, parts)
    grad_att = exchange(grad_att)
    grad_att, two_came, feed_grads, out_grads = fence((grad_att, two_came, feed_grads, out_grads))
    onward = sent(added(feed_grads, 2, two_came), "z", 1)
    three_came = crossed(feed_grads, 3)
    if parts == 2:
        out_sums = out_grads[0].astype(F32) + swap(out_grads[1], "y").astype(F32)
    else:
        out_sums = lax.psum_scatter(out_grads[0], "y", scatter_dimension=2, tiled=True)
    dq, keep, give = attend_back(ids, q_seq, kv_seq, o_seq, lse, cosine, sine, grad_att)
    dq, keep, give, onward, three_came, feed_grads, ffn_near, ffn_far, out_sums = fence(
        (dq, keep, give, onward, three_came, feed_grads, ffn_near, ffn_far, out_sums.astype(BF16))
    )
    one_came = crossed(feed_grads, 1)
    grads_heads = exchange(pack(ids, dq, keep, swap(give, "c")))
    branch_ffn = scatter_halves(ffn_near, ffn_far)
    result = state + branch_ffn
    squares = jnp.stack([jnp.sum(result * result), jnp.sum(branch_attn * branch_attn), jnp.sum(branch_ffn * branch_ffn)])
    squares = squares + swap(squares, "c")
    squares = squares + swap(squares, "x")
    onward = (added(feed_grads, 3, three_came).astype(F32) + onward.astype(F32)).astype(BF16)
    onward, onward_down = onward[:2], onward[2:]
    one_sum = added(feed_grads, 1, one_came)
    grads_heads, result, squares, onward, onward_down, one_sum, feed_grads = fence(
        (grads_heads, result, squares, onward, onward_down, one_sum, feed_grads)
    )
    onward = sent(onward, "z", 3)
    grads_qkv, qkv_grads = project_weights(ids, grads_heads, x_one, parts)
    grads_qkv, qkv_grads = fence((grads_qkv, qkv_grads))
    near, far = project_tokens(ids, grads_qkv, attn_weights)
    if parts == 2:
        late, early = (kept.astype(F32) + swap(gone, "y").astype(F32) for kept, gone in zip(qkv_grads[:2], qkv_grads[2:]))
    else:
        late, early = (lax.psum_scatter(piece, "y", scatter_dimension=2, tiled=True) for piece in qkv_grads)
    sums = [early[0], early[1], late[0], late[1]]
    sums = [jnp.concatenate([sums[k].astype(BF16), out_sums[k]], axis=0) for k in range(4)]
    sums, feed_grads, onward, onward_down = fence((sums, feed_grads, onward, onward_down))
    onward_down = sent(onward_down, "z", 3)
    own_came = crossed(feed_grads, 0)
    onto_three = (sums[3].astype(F32) + sent(sums[2], "z", 1).astype(F32)).astype(BF16)
    onto_one = sent(sums[1], "z", 1)
    total = near.astype(F32) + swap(far, "c").astype(F32)
    onto_three, onto_one, total, onward_down, one_sum = fence((onto_three, onto_one, total, onward_down, one_sum))
    onto_three = sent(onto_three, "z", 3)
    feed_one = sent(one_sum, "z", 1)
    crossing = swap(total[1].astype(BF16), "x")
    feed_total = added(feed_grads, 0, own_came).astype(F32) + jnp.concatenate([onward, onward_down]).astype(F32)
    feed_total = feed_total + feed_one.astype(F32)
    squares = squares + swap(squares, "y") if parts == 2 else lax.psum(squares, "y")
    onto_three, crossing, feed_total = fence((onto_three, crossing, feed_total.astype(BF16)))
    attn_total = sums[0].astype(F32) + onto_one.astype(F32) + onto_three.astype(F32)
    grad_unit_one = total[0] + crossing.astype(F32)
    grad_tokens = (grad_state + unit_back(resid, scale_one, grad_unit_one)).astype(BF16)
    grad_gate, grad_up, grad_down, gain_two = finish_ffn(ids, home(feed_total), w_gate, w_up, gain_ffn)
    grad_query, grad_key, grad_value, grad_outproj, gain_one = finish_attn(
        ids, home_lanes(attn_total.astype(BF16)), w_query, w_key, w_value, gain_attn
    )
    sums = over_z(jnp.concatenate([gain_one[0], gain_two[0], squares]))
    entries = block * width * sequences * SPANS * count
    return (
        result.astype(BF16),
        grad_tokens,
        grad_query,
        grad_key,
        grad_value,
        grad_outproj.T,
        grad_gate,
        grad_up,
        grad_down.T,
        sums[:shard],
        sums[shard : 2 * shard],
        jnp.sqrt(sums[2 * shard :] / entries),
    )


def solution(mesh):
    fsdp, tensor = mesh.shape["fsdp"], mesh.shape["tensor"]
    split = Mesh(mesh.devices.reshape(fsdp // SPANS, 2, 2, tensor), ("y", "x", "c", "z"))
    rows = ("y", "x", "c")
    tok = P(("y", "x", "c", "z"), None)
    col, row, vec = P(rows, "z"), P("z", rows), P(rows)
    return jax.shard_map(
        per_device,
        mesh=split,
        in_specs=(tok, col, col, col, row, col, col, row, vec, vec, tok),
        out_specs=(tok, tok, col, col, col, row, col, col, row, vec, vec, P()),
        check_vma=False,
    )
```

time: 845 us -> 618 us (0.73)
  waiting for transfers between devices: 398 us -> 284 us
  blocking collectives: 93.9 us -> 0 us
  Pallas kernels: 97.1 us -> 165 us
  local copies, waits for them, and re-layouts: 83.4 us -> 18.3 us
  matrix products: 49.9 us -> 0 us
  starting transfers between devices: 58.6 us -> 88.5 us
  between operations: 14.9 us -> 1.78 us
    reduce_scatter x2 -> x0, waiting for transfers between devices: 115 us -> none  [the longest x1 115 us: settle(): lax.psum_scatter(grads, ('y', 'z'), scatter_dimension=0, tiled=False)]
    pallas_call x5 -> x13, Pallas kernels: 36.3 us -> 105 us  [run(): pl.pallas_call(kernel, out_shape=[shape(*o) if isinstance(o[0], tuple) el...]
    psum x2 -> x0, blocking collectives: 61.7 us -> none  [the longest x1 51.7 us: per_device(): squares = lax.psum(squares, ('y', 'x', 'c', 'z'))]
    ppermute x22 -> x50, waiting for transfers between devices: 126 us -> 180 us  [swap(): return lax.ppermute(value, axis, [(0, 1), (1, 0)])]
    dot_general x9 -> x0, matrix products: 49.9 us -> none  [the longest x6 30.7 us: mm(): return lax.dot_general(left, right, dims, preferred_element_type=F32)]
    ppermute x15 -> x23, waiting for transfers between devices: 125 us -> 87.3 us  [the longest x19 78.3 us: sent(): lax.ppermute(value, axis, [(i, i ^ bits) for i in range(lax.axis_size(axi...]
    another operation x14 -> x0, local copies, waits for them, and re-layouts: 33.7 us -> none  [the longest x6 25.8 us: per_device(): jnp.stack([mm(x_two, grad_gate_pre, TN).astype(BF16), mm(x_two, grad_up_p...]
    all_to_all x2 -> x0, blocking collectives: 32.1 us -> none  [spread(): lax.all_to_all(payload, ('x', 'c'), split_axis=0, concat_axis=0, tiled=True)]
  transfers between devices with their start and end apart: 43 -> 77, of which waited for: 26 -> 41; matrix products, arithmetic and copies ran while one was open for 14% -> 7% of each run, Pallas kernels for 5% -> 21%
where the time goes in v2:
time: 618 us; the launch traced here: 609 us
  waiting for transfers between devices  284 us (46%)
  Pallas kernels  165 us (27%)
  starting transfers between devices  88.5 us (14%)
  other arithmetic  50.9 us (8%)
  local copies, waits for them, and re-layouts  18.3 us (3%)
    ppermute x50, waiting for transfers between devices, swap(): return lax.ppermute(value, axis, [(0, 1), (1, 0)])  180 us
    pallas_call x13, Pallas kernels, run(): pl.pallas_call(kernel, out_shape=[shape(*o) if isinstance(o[0], tuple) el...  105 us
    ppermute x19, waiting for transfers between devices, sent(): lax.ppermute(value, axis, [(i, i ^ bits) for i in range(lax.axis_size(axi...  78.3 us
    ppermute x50, starting transfers between devices, swap(): return lax.ppermute(value, axis, [(0, 1), (1, 0)])  39.9 us
    pallas_call x1, Pallas kernels, attend_back(): pl.pallas_call(functools.partial(attend_back_kernel, block=block, tile=ti...  38.9 us
    ppermute x19, starting transfers between devices, sent(): lax.ppermute(value, axis, [(i, i ^ bits) for i in range(lax.axis_size(axi...  30.8 us
    pallas_call x1, Pallas kernels, attend(): pl.pallas_call(functools.partial(attend_kernel, block=block, tile=tile),...  20.9 us
    all_to_all x4, waiting for transfers between devices, exchange(): return lax.all_to_all(pieces, 'z', split_axis=0, concat_axis=0, tiled=True)  17.1 us
  transfers between devices with their start and end apart: 77, of which 41 were waited for; matrix products, arithmetic and copies ran while one was open for 7% of the time, Pallas kernels for 21%

profile of v2, /device:TPU:0, one launch (start us, length us, event | category | flops | bytes accessed | tf_op | source)
XLA Modules:
  0.0 608.7 jit_solution(17550781426423411310)
XLA Ops:
  36.5 11.6 %collective-permute-done.6 = bf16[288,768]{1,0:T(8,128)(2,1)S(1)} collective-permute-done((bf16[288,768]{1,0:T(8,128)(2,1)S(1)}, bf16[288,768]{1,0:T(8,128)(2,1)S(1)}, u32[]{:S(2)}, u32[]{:S(2)}) %collective-permute-start.6) | collective-permute-done | bytes 442400 | tf_op jit(solution)/shard_map/ppermute | solution.py:557
  53.6 13.7 %collective-permute-done.13.refs_2_.refs_3_ = bf16[256,1536]{1,0:T(8,128)(2,1)S(1)} collective-permute-done((bf16[256,1536]{1,0:T(8,128)(2,1)S(1)}, bf16[256,1536]{1,0:T(8,128)(2,1)S(1)}, u32[]{:S(2)}, u32[]{:S(2)}) %collective-permute-start.13) | collective-permute-done | bytes 786464 | tf_op jit(solution)/shard_map/ppermute | solution.py:553
  77.3 8.9 %collective-permute-done.15.refs_9_.refs_6_ = bf16[288,768]{1,0:T(8,128)(2,1)S(1)} collective-permute-done((bf16[288,768]{1,0:T(8,128)(2,1)S(1)}, bf16[288,768]{1,0:T(8,128)(2,1)S(1)}, u32[]{:S(2)}, u32[]{:S(2)}) %collective-permute-start.15) | collective-permute-done | bytes 442400 | tf_op jit(solution)/shard_map/ppermute | solution.py:553
  87.0 10.0 %project.1 = bf16[4,256,768]{2,1,0:T(8,128)(2,1)} custom-call(s32[3]{0:T(128)} %pad_add_fusion.ids, bf16[256,1536]{1,0:T(8,128)(2,1)} %copy-done.6, bf16[256,1536]{1,0:T(8,128)(2,1)} %copy-done.13, bf16[256,1536]{1,0:T(8,128)(2,1)} %copy-done.12, bf16[256,1536]{1,0:T(8,128)(2,1)} %collective-permute-done.14.refs_3_.refs_4_, bf16[288,768]{1,0:T(8,128)(2,1)} %copy-done.7, ...), custom_call_target="tpu_custom_call" | custom-call | flops 1 | bytes 1 | tf_op jit(solution)/shard_map/project/pallas_call | solution.py:220
  103.9 17.4 %collective-permute-done.20.refs_2_.refs_6_ = bf16[256,1536]{1,0:T(8,128)(2,1)S(1)} collective-permute-done((bf16[256,1536]{1,0:T(8,128)(2,1)}, bf16[256,1536]{1,0:T(8,128)(2,1)S(1)}, u32[]{:S(2)}, u32[]{:S(2)}) %collective-permute-start.20) | collective-permute-done | bytes 786464 | tf_op jit(solution)/shard_map/ppermute | solution.py:553
  124.0 5.8 collective-permute-done.18.refs_9_
  130.8 8.1 %all-to-all-done.own = bf16[4,256,768]{2,1,0:T(8,128)(2,1)S(1)} async-done(((bf16[4,256,768]{2,1,0:T(8,128)(2,1)}), bf16[4,256,768]{2,1,0:T(8,128)(2,1)S(1)}, u32[]{:S(2)}, u32[]{:S(2)}) %all-to-all-start) | async-done | bytes 1572896 | tf_op jit(solution)/shard_map/all_to_all | solution.py:578
  142.1 20.9 %attend.1 = (bf16[4,256,384]{2,1,0:T(8,128)(2,1)}, bf16[4096,128]{1,0:T(8,128)(2,1)}, bf16[2,4096,128]{2,1,0:T(8,128)(2,1)}, bf16[4096,128]{1,0:T(8,128)(2,1)}, f32[8,4096]{1,0:T(8,128)}) custom-call(s32[3]{0:T(128)} %pad_add_fusion.ids, bf16[4,256,768]{2,1,0:T(8,128)(2,1)} %copy-done.11, bf16[4,256,384]{2,1,0:T(8,128)(2,1)} %collective-permute-done.22.other), custom_call_target="tpu_custom_call" | custom-call | flops 20999999488 | bytes 1 | tf_op jit(solution)/shard_map/attend/pallas_call | solution.py:106
  163.0 5.8 collective-permute-done.24
  176.2 16.5 %collective-permute-done.26.refs_11_ = bf16[2,768,256]{2,1,0:T(8,128)(2,1)} collective-permute-done((bf16[2,768,256]{2,1,0:T(8,128)(2,1)S(1)}, bf16[2,768,256]{2,1,0:T(8,128)(2,1)}, u32[]{:S(2)}, u32[]{:S(2)}) %collective-permute-start.26) | collective-permute-done | bytes 786464 | tf_op jit(solution)/shard_map/ppermute | solution.py:553
  194.4 5.5 out_project.1
  208.6 16.5 %collective-permute-done.28 = bf16[256,1536]{1,0:T(8,128)(2,1)S(1)} collective-permute-done((bf16[256,1536]{1,0:T(8,128)(2,1)S(1)}, bf16[256,1536]{1,0:T(8,128)(2,1)S(1)}, u32[]{:S(2)}, u32[]{:S(2)}) %collective-permute-start.28) | collective-permute-done | bytes 786464 | tf_op jit(solution)/shard_map/ppermute | solution.py:553
  226.6 7.2 %collective-permute-done.29.refs_8_ = bf16[3,768,256]{2,1,0:T(8,128)(2,1)S(1)} collective-permute-done((bf16[3,768,256]{2,1,0:T(8,128)(2,1)S(1)}, bf16[3,768,256]{2,1,0:T(8,128)(2,1)S(1)}, u32[]{:S(2)}, u32[]{:S(2)}) %collective-permute-start.29) | collective-permute-done | bytes 1179680 | tf_op jit(solution)/shard_map/ppermute | solution.py:557
  236.8 15.4 %collective-permute-done.32.refs_0_.refs_2_ = bf16[256,1536]{1,0:T(8,128)(2,1)S(1)} collective-permute-done((bf16[256,1536]{1,0:T(8,128)(2,1)S(1)}, bf16[256,1536]{1,0:T(8,128)(2,1)S(1)}, u32[]{:S(2)}, u32[]{:S(2)}) %collective-permute-start.32) | collective-permute-done | bytes 786464 | tf_op jit(solution)/shard_map/ppermute | solution.py:553
  252.3 9.6 %collective-permute-done.34.refs_13_ = bf16[3,768,256]{2,1,0:T(8,128)(2,1)S(1)} collective-permute-done((bf16[3,768,256]{2,1,0:T(8,128)(2,1)S(1)}, bf16[3,768,256]{2,1,0:T(8,128)(2,1)S(1)}, u32[]{:S(2)}, u32[]{:S(2)}) %collective-permute-start.34) | collective-permute-done | bytes 1179680 | tf_op jit(solution)/shard_map/ppermute | solution.py:553
  262.9 18.7 %feed.2 = (bf16[256,1536]{1,0:T(8,128)(2,1)}, bf16[256,1536]{1,0:T(8,128)(2,1)}, bf16[256,1536]{1,0:T(8,128)(2,1)}, bf16[256,1536]{1,0:T(8,128)(2,1)}, bf16[512,...) custom-call(s32[3]{0:T(128)} %pad_add_fusion.ids, bf16[256,1536]{1,0:T(8,128)(2,1)} %copy-done.54, ...), custom_call_target="tpu_custom_call" | custom-call | flops 18000001024 | bytes 1 | tf_op jit(solution)/shard_map/feed/pallas_call | solution.py:220
  286.9 18.8 %feed.3 = (bf16[256,1536]{1,0:T(8,128)(2,1)}, bf16[256,1536]{1,0:T(8,128)(2,1)}, bf16[256,1536]{1,0:T(8,128)(2,1)}, bf16[256,1536]{1,0:T(8,128)(2,1)}, bf16[512,...) custom-call(s32[3]{0:T(128)} %pad_add_fusion.ids, bf16[256,1536]{1,0:T(8,128)(2,1)} %copy-done.33, ...), custom_call_target="tpu_custom_call" | custom-call | flops 18000001024 | bytes 1 | tf_op jit(solution)/shard_map/feed/pallas_call | solution.py:220
  314.8 16.9 %feed_weights.1 = (bf16[3,768,256]{2,1,0:T(8,128)(2,1)}, bf16[3,768,256]{2,1,0:T(8,128)(2,1)}, bf16[3,768,256]{2,1,0:T(8,128)(2,1)}, bf16[3,768,256]{2,1,0:T(8,1...) custom-call(s32[3]{0:T(128)} %pad_add_fusion.ids, ...), custom_call_target="tpu_custom_call" | custom-call | flops 17000000512 | bytes 1 | tf_op jit(solution)/shard_map/feed_weights/pallas_call | solution.py:220
  336.4 6.4 %out_back.1 = (bf16[4,256,384]{2,1,0:T(8,128)(2,1)}, bf16[4,96,768]{2,1,0:T(8,128)(2,1)}, bf16[4,96,768]{2,1,0:T(8,128)(2,1)}) custom-call(s32[3]{0:T(128)} %pad_add_fusion.ids, bf16[256,1536]{1,0:T(8,128)(2,1)} %get-tuple-element.303.refs_0_, bf16[256,1536]{1,0:T(8,128)(2,1)} %copy-done.34, bf16[256,1536]{1,0:T(8,128)(2,1)} %collective-permute-done.38.refs_2_, ...), custom_call_target="tpu_custom_call" | custom-call | flops 1 | bytes 1 | tf_op jit(solution)/shard_map/out_back/pallas_call | solution.py:220
  347.2 15.3 %collective-permute-done.41 = bf16[3,768,256]{2,1,0:T(8,128)(2,1)} collective-permute-done((bf16[3,768,256]{2,1,0:T(8,128)(2,1)}, bf16[3,768,256]{2,1,0:T(8,128)(2,1)}, u32[]{:S(2)}, u32[]{:S(2)}) %collective-permute-start.41) | collective-permute-done | bytes 1179680 | tf_op jit(solution)/shard_map/ppermute | solution.py:553
  362.4 5.5 all-to-all-done.2.g
  372.5 38.9 %attend_back.1 = (bf16[4,256,384]{2,1,0:T(8,128)(2,1)}, bf16[4096,128]{1,0:T(8,128)(2,1)}, bf16[4096,128]{1,0:T(8,128)(2,1)}) custom-call(s32[3]{0:T(128)} %pad_add_fusion.ids, bf16[4096,128]{1,0:T(8,128)(2,1)} %get-tuple-element.248.q_s, bf16[2,4096,128]{2,1,0:T(8,128)(2,1)} %get-tuple-element.249.kv_s, bf16[4096,128]{1,0:T(8,128)(2,1)} %get-tuple-element.250.o_s, ...), custom_call_target="tpu_custom_call" | custom-call | flops 38999998464 | bytes 1 | tf_op jit(solution)/shard_map/attend_back/pallas_call | solution.py:192
  431.4 10.2 %collective-permute-done.51 = bf16[3,768,256]{2,1,0:T(8,128)(2,1)} collective-permute-done((bf16[3,768,256]{2,1,0:T(8,128)(2,1)}, bf16[3,768,256]{2,1,0:T(8,128)(2,1)}, u32[]{:S(2)}, u32[]{:S(2)}) %collective-permute-start.51) | collective-permute-done | bytes 1179680 | tf_op jit(solution)/shard_map/ppermute | solution.py:553
  461.7 7.6 %project_weights.1 = (bf16[1024,768]{1,0:T(8,128)(2,1)}, bf16[2,192,768]{2,1,0:T(8,128)(2,1)}, bf16[2,192,768]{2,1,0:T(8,128)(2,1)}, bf16[2,192,768]{2,1,0:T(8,128)(2,1)}, bf16[2,192,768]{2,1,0:T(8,128)(2,1)}) custom-call(s32[3]{0:T(128)} %pad_add_fusion.ids, bf16[4,256,768]{2,1,0:T(8,128)(2,1)} %all-to-all-done.3.refs_0_, bf16[256,1536]{1,0:T(8,128)(2,1)} %copy-done.6, ...), custom_call_target="tpu_custom_call" | custom-call | flops 1 | bytes 1 | tf_op jit(solution)/shard_map/project_weights/pallas_call | solution.py:220
  473.2 6.5 %project_tokens.1 = (bf16[2,256,1536]{2,1,0:T(8,128)(2,1)}, bf16[2,256,1536]{2,1,0:T(8,128)(2,1)}) custom-call(s32[3]{0:T(128)} %pad_add_fusion.ids, bf16[1024,768]{1,0:T(8,128)(2,1)} %get-tuple-element.379.refs_0_, bf16[288,768]{1,0:T(8,128)(2,1)} %copy-done.7, bf16[288,768]{1,0:T(8,128)(2,1)} %copy-done.8, bf16[2,288,768]{2,1,0:T(8,128)(2,1)} %copy-done.3, ...), custom_call_target="tpu_custom_call" | custom-call | flops 1 | bytes 1 | tf_op jit(solution)/shard_map/project_tokens/pallas_call | solution.py:220
  479.7 6.2 %collective-permute-done.52 = bf16[2,192,768]{2,1,0:T(8,128)(2,1)} collective-permute-done((bf16[2,192,768]{2,1,0:T(8,128)(2,1)}, bf16[2,192,768]{2,1,0:T(8,128)(2,1)}, u32[]{:S(2)}, u32[]{:S(2)}) %collective-permute-start.52) | collective-permute-done | bytes 589856 | tf_op jit(solution)/shard_map/ppermute | solution.py:553
  487.2 9.6 %collective-permute-done.53 = bf16[2,192,768]{2,1,0:T(8,128)(2,1)} collective-permute-done((bf16[2,192,768]{2,1,0:T(8,128)(2,1)}, bf16[2,192,768]{2,1,0:T(8,128)(2,1)}, u32[]{:S(2)}, u32[]{:S(2)}) %collective-permute-start.53) | collective-permute-done | bytes 589856 | tf_op jit(solution)/shard_map/ppermute | solution.py:553
  498.2 7.6 %collective-permute-start.55 = (bf16[288,768]{1,0:T(8,128)(2,1)S(1)}, bf16[288,768]{1,0:T(8,128)(2,1)S(1)}, u32[]{:S(2)}, u32[]{:S(2)}) collective-permute-start(bf16[288,768]{1,0:T(8,128)(2,1)S(1)} %get-tuple-element.377), channel_id=1, source_target_pairs={{0,1},{1,0},{2,3},{3,2},{4,5},{5,4},{6,7},{7,6},{8,9},{9,8},{10,11... | collective-permute-start | bytes 1327112 | tf_op jit(solution)/shard_map/ppermute | solution.py:557
  509.4 13.9 %collective-permute-done.55 = bf16[288,768]{1,0:T(8,128)(2,1)S(1)} collective-permute-done((bf16[288,768]{1,0:T(8,128)(2,1)S(1)}, bf16[288,768]{1,0:T(8,128)(2,1)S(1)}, u32[]{:S(2)}, u32[]{:S(2)}) %collective-permute-start.55) | collective-permute-done | bytes 442400 | tf_op jit(solution)/shard_map/ppermute | solution.py:557
  540.9 19.6 %collective-permute-done.62 = bf16[3,768,256]{2,1,0:T(8,128)(2,1)S(1)} collective-permute-done((bf16[3,768,256]{2,1,0:T(8,128)(2,1)S(1)}, bf16[3,768,256]{2,1,0:T(8,128)(2,1)S(1)}, u32[]{:S(2)}, u32[]{:S(2)}) %collective-permute-start.62) | collective-permute-done | bytes 1179680 | tf_op jit(solution)/shard_map/ppermute | solution.py:557
  561.1 7.0 %collective-permute-done.59 = bf16[288,768]{1,0:T(8,128)(2,1)S(1)} collective-permute-done((bf16[288,768]{1,0:T(8,128)(2,1)S(1)}, bf16[288,768]{1,0:T(8,128)(2,1)S(1)}, u32[]{:S(2)}, u32[]{:S(2)}) %collective-permute-start.59) | collective-permute-done | bytes 442400 | tf_op jit(solution)/shard_map/ppermute | solution.py:557
  577.7 10.7 %collective-permute-done.64.refs_2_ = bf16[288,192]{1,0:T(8,128)(2,1)} collective-permute-done((bf16[288,192]{1,0:T(8,128)(2,1)S(1)}, bf16[288,192]{1,0:T(8,128)(2,1)}, u32[]{:S(2)}, u32[]{:S(2)}) %collective-permute-start.64) | collective-permute-done | bytes 110624 | tf_op jit(solution)/shard_map/ppermute | solution.py:553
  (340 shorter events, 214.6 us)
Async XLA Ops:
  25.8 22.3 %collective-permute-start.6 = (bf16[288,768]{1,0:T(8,128)(2,1)S(1)}, bf16[288,768]{1,0:T(8,128)(2,1)S(1)}, u32[]{:S(2)}, u32[]{:S(2)}) collective-permute-start(bf16[288,768]{1,0:T(8,128)(2,1)S(1)} %reshape.204.refs_4_.refs_1_), channel_id=1, source_target_pairs={{0,3},{1,2},{2,1},{3,0},{4,7},{5,6},{6,5},{7,4},{8,11},{9,10},{10,... | collective-permute-start | bytes 1327112 | tf_op jit(solution)/shard_map/ppermute | solution.py:557
  48.2 24.3 %collective-permute-start.10 = (bf16[2,288,768]{2,1,0:T(8,128)(2,1)S(1)}, bf16[2,288,768]{2,1,0:T(8,128)(2,1)S(1)}, u32[]{:S(2)}, u32[]{:S(2)}) collective-permute-start(bf16[2,288,768]{2,1,0:T(8,128)(2,1)S(1)} %pad_maximum_fusion.2.refs_6_.refs_3_), channel_id=1, source_target_pairs={{0,16},{16,0},{1,17},{17,1},{2,18},{18,2},{3,19},{19,3},{4,20},{20... | collective-permute-start | bytes 2654216 | tf_op jit(solution)/shard_map/ppermute | solution.py:553
  50.3 22.2 %collective-permute-start.9 = (bf16[288,768]{1,0:T(8,128)(2,1)S(1)}, bf16[288,768]{1,0:T(8,128)(2,1)S(1)}, u32[]{:S(2)}, u32[]{:S(2)}) collective-permute-start(bf16[288,768]{1,0:T(8,128)(2,1)S(1)} %collective-permute-done.6), channel_id=1, source_target_pairs={{0,1},{1,0},{2,3},{3,2},{4,5},{5,4},{6,7},{7,6},{8,9},{9,8},{10,11... | collective-permute-start | bytes 1327112 | tf_op jit(solution)/shard_map/ppermute | solution.py:557
  50.9 21.6 %collective-permute-start.11 = (bf16[768,256]{1,0:T(8,128)(2,1)S(1)}, bf16[768,256]{1,0:T(8,128)(2,1)S(1)}, u32[]{:S(2)}, u32[]{:S(2)}) collective-permute-start(bf16[768,256]{1,0:T(8,128)(2,1)S(1)} %slice_bitcast_fusion.4), channel_id=1, source_target_pairs={{0,3},{1,2},{2,1},{3,0},{4,7},{5,6},{6,5},{7,4},{8,11},{9,10},{10,... | collective-permute-start | bytes 1179656 | tf_op jit(solution)/shard_map/ppermute | solution.py:557
  97.7 41.2 %all-to-all-start = ((bf16[4,256,768]{2,1,0:T(8,128)(2,1)}), bf16[4,256,768]{2,1,0:T(8,128)(2,1)S(1)}, u32[]{:S(2)}, u32[]{:S(2)}) async-start(bf16[4,256,768]{2,1,0:T(8,128)(2,1)} %project.1), calls=%async_computation | async-start | bytes 3145728 | tf_op jit(solution)/shard_map/all_to_all | solution.py:578
  102.4 27.4 %collective-permute-start.18 = (bf16[3,768,256]{2,1,0:T(8,128)(2,1)S(1)}, bf16[3,768,256]{2,1,0:T(8,128)(2,1)S(1)}, u32[]{:S(2)}, u32[]{:S(2)}) collective-permute-start(bf16[3,768,256]{2,1,0:T(8,128)(2,1)S(1)} %bitcast.113), channel_id=1, source_target_pairs={{0,16},{16,0},{1,17},{17,1},{2,18},{18,2},{3,19},{19,3},{4,20},{20... | collective-permute-start | bytes 3538952 | tf_op jit(solution)/shard_map/ppermute | solution.py:553
  139.1 23.9 %collective-permute-start.23 = (bf16[768,256]{1,0:T(8,128)(2,1)S(1)}, bf16[768,256]{1,0:T(8,128)(2,1)S(1)}, u32[]{:S(2)}, u32[]{:S(2)}) collective-permute-start(bf16[768,256]{1,0:T(8,128)(2,1)S(1)} %get-tuple-element.253), channel_id=1, source_target_pairs={{0,3},{1,2},{2,1},{3,0},{4,7},{5,6},{6,5},{7,4},{8,11},{9,10},{10,... | collective-permute-start | bytes 1179656 | tf_op jit(solution)/shard_map/ppermute | solution.py:557
  140.6 28.2 %collective-permute-start.24 = (bf16[2,768,256]{2,1,0:T(8,128)(2,1)}, bf16[2,768,256]{2,1,0:T(8,128)(2,1)S(1)}, u32[]{:S(2)}, u32[]{:S(2)}) collective-permute-start(bf16[2,768,256]{2,1,0:T(8,128)(2,1)} %get-tuple-element.254), channel_id=1, source_target_pairs={{0,1},{1,0},{2,3},{3,2},{4,5},{5,4},{6,7},{7,6},{8,9},{9,8},{10,11... | collective-permute-start | bytes 2359304 | tf_op jit(solution)/shard_map/ppermute | solution.py:557
  140.6 28.2 %collective-permute-start.25 = (bf16[2,768,256]{2,1,0:T(8,128)(2,1)}, bf16[2,768,256]{2,1,0:T(8,128)(2,1)}, u32[]{:S(2)}, u32[]{:S(2)}) collective-permute-start(bf16[2,768,256]{2,1,0:T(8,128)(2,1)} %get-tuple-element.273.refs_5_), channel_id=1, source_target_pairs={{0,16},{16,0},{1,17},{17,1},{2,18},{18,2},{3,19},{19,3},{4,20},{20... | collective-permute-start | bytes 2359304 | tf_op jit(solution)/shard_map/ppermute | solution.py:553
  169.7 23.7 %all-to-all-start.1 = ((bf16[4,256,384]{2,1,0:T(8,128)(2,1)}), bf16[4,256,384]{2,1,0:T(8,128)(2,1)S(1)}, u32[]{:S(2)}, u32[]{:S(2)}) async-start(bf16[4,256,384]{2,1,0:T(8,128)(2,1)} %get-tuple-element.257), calls=%async_computation.1 | async-start | bytes 1572864 | tf_op jit(solution)/shard_map/all_to_all | solution.py:578
  206.1 27.7 %collective-permute-start.29 = (bf16[3,768,256]{2,1,0:T(8,128)(2,1)S(1)}, bf16[3,768,256]{2,1,0:T(8,128)(2,1)S(1)}, u32[]{:S(2)}, u32[]{:S(2)}) collective-permute-start(bf16[3,768,256]{2,1,0:T(8,128)(2,1)S(1)} %pad_maximum_fusion.1), channel_id=1, source_target_pairs={{0,1},{1,0},{2,3},{3,2},{4,5},{5,4},{6,7},{7,6},{8,9},{9,8},{10,11... | collective-permute-start | bytes 3538952 | tf_op jit(solution)/shard_map/ppermute | solution.py:557
  235.3 26.6 %collective-permute-start.34 = (bf16[3,768,256]{2,1,0:T(8,128)(2,1)S(1)}, bf16[3,768,256]{2,1,0:T(8,128)(2,1)S(1)}, u32[]{:S(2)}, u32[]{:S(2)}) collective-permute-start(bf16[3,768,256]{2,1,0:T(8,128)(2,1)S(1)} %collective-permute-done.29.refs_8_), channel_id=1, source_target_pairs={{0,16},{16,0},{1,17},{17,1},{2,18},{18,2},{3,19},{19,3},{4,20},{20... | collective-permute-start | bytes 3538952 | tf_op jit(solution)/shard_map/ppermute | solution.py:553
  333.7 28.7 %collective-permute-start.41 = (bf16[3,768,256]{2,1,0:T(8,128)(2,1)}, bf16[3,768,256]{2,1,0:T(8,128)(2,1)}, u32[]{:S(2)}, u32[]{:S(2)}) collective-permute-start(bf16[3,768,256]{2,1,0:T(8,128)(2,1)} %get-tuple-element.323), channel_id=1, source_target_pairs={{0,16},{16,0},{1,17},{17,1},{2,18},{18,2},{3,19},{19,3},{4,20},{20... | collective-permute-start | bytes 3538952 | tf_op jit(solution)/shard_map/ppermute | solution.py:553
  342.8 25.1 %all-to-all-start.2 = ((bf16[4,256,384]{2,1,0:T(8,128)(2,1)}), bf16[4,256,384]{2,1,0:T(8,128)(2,1)}, u32[]{:S(2)}, u32[]{:S(2)}) async-start(bf16[4,256,384]{2,1,0:T(8,128)(2,1)} %get-tuple-element.322), calls=%async_computation.2 | async-start | bytes 1572864 | tf_op jit(solution)/shard_map/all_to_all | solution.py:578
  367.9 43.6 %collective-permute-start.44 = (bf16[4,96,768]{2,1,0:T(8,128)(2,1)}, bf16[4,96,768]{2,1,0:T(8,128)(2,1)}, u32[]{:S(2)}, u32[]{:S(2)}) collective-permute-start(bf16[4,96,768]{2,1,0:T(8,128)(2,1)} %get-tuple-element.350), channel_id=1, source_target_pairs={{0,16},{16,0},{1,17},{17,1},{2,18},{18,2},{3,19},{19,3},{4,20},{20... | collective-permute-start | bytes 1769480 | tf_op jit(solution)/shard_map/ppermute | solution.py:553
  372.0 40.8 %collective-permute-start.42 = (bf16[3,768,256]{2,1,0:T(8,128)(2,1)}, bf16[3,768,256]{2,1,0:T(8,128)(2,1)}, u32[]{:S(2)}, u32[]{:S(2)}) collective-permute-start(bf16[3,768,256]{2,1,0:T(8,128)(2,1)} %add_convert_fusion.5), channel_id=1, source_target_pairs={{0,1},{1,0},{2,3},{3,2},{4,5},{5,4},{6,7},{7,6},{8,9},{9,8},{10,11... | collective-permute-start | bytes 3538952 | tf_op jit(solution)/shard_map/ppermute | solution.py:557
  372.0 40.8 %collective-permute-start.43 = (bf16[3,768,256]{2,1,0:T(8,128)(2,1)}, bf16[3,768,256]{2,1,0:T(8,128)(2,1)}, u32[]{:S(2)}, u32[]{:S(2)}) collective-permute-start(bf16[3,768,256]{2,1,0:T(8,128)(2,1)} %get-tuple-element.339), channel_id=1, source_target_pairs={{0,16},{16,0},{1,17},{17,1},{2,18},{18,2},{3,19},{19,3},{4,20},{20... | collective-permute-start | bytes 3538952 | tf_op jit(solution)/shard_map/ppermute | solution.py:553
  413.4 28.3 %collective-permute-start.51 = (bf16[3,768,256]{2,1,0:T(8,128)(2,1)}, bf16[3,768,256]{2,1,0:T(8,128)(2,1)}, u32[]{:S(2)}, u32[]{:S(2)}) collective-permute-start(bf16[3,768,256]{2,1,0:T(8,128)(2,1)} %get-tuple-element.362), channel_id=1, source_target_pairs={{0,16},{16,0},{1,17},{17,1},{2,18},{18,2},{3,19},{19,3},{4,20},{20... | collective-permute-start | bytes 3538952 | tf_op jit(solution)/shard_map/ppermute | solution.py:553
  419.8 42.0 %all-to-all-start.3 = ((bf16[4,256,768]{2,1,0:T(8,128)(2,1)}), bf16[4,256,768]{2,1,0:T(8,128)(2,1)}, u32[]{:S(2)}, u32[]{:S(2)}) async-start(bf16[4,256,768]{2,1,0:T(8,128)(2,1)} %pack.1), calls=%async_computation.3 | async-start | bytes 3145728 | tf_op jit(solution)/shard_map/all_to_all | solution.py:578
  470.9 25.9 %collective-permute-start.53 = (bf16[2,192,768]{2,1,0:T(8,128)(2,1)}, bf16[2,192,768]{2,1,0:T(8,128)(2,1)}, u32[]{:S(2)}, u32[]{:S(2)}) collective-permute-start(bf16[2,192,768]{2,1,0:T(8,128)(2,1)} %get-tuple-element.371), channel_id=1, source_target_pairs={{0,16},{16,0},{1,17},{17,1},{2,18},{18,2},{3,19},{19,3},{4,20},{20... | collective-permute-start | bytes 1769480 | tf_op jit(solution)/shard_map/ppermute | solution.py:553
  471.5 26.7 %collective-permute-start.54 = (bf16[2,768,256]{2,1,0:T(8,128)(2,1)S(1)}, bf16[2,768,256]{2,1,0:T(8,128)(2,1)S(1)}, u32[]{:S(2)}, u32[]{:S(2)}) collective-permute-start(bf16[2,768,256]{2,1,0:T(8,128)(2,1)S(1)} %copy-done.28), channel_id=1, source_target_pairs={{0,3},{1,2},{2,1},{3,0},{4,7},{5,6},{6,5},{7,4},{8,11},{9,10},{10,... | collective-permute-start | bytes 2359304 | tf_op jit(solution)/shard_map/ppermute | solution.py:557
  479.7 43.7 %collective-permute-start.57 = (bf16[2,256,1536]{2,1,0:T(8,128)(2,1)}, bf16[2,256,1536]{2,1,0:T(8,128)(2,1)S(1)}, u32[]{:S(2)}, u32[]{:S(2)}) collective-permute-start(bf16[2,256,1536]{2,1,0:T(8,128)(2,1)} %get-tuple-element.381), channel_id=1, source_target_pairs={{0,4},{4,0},{1,5},{5,1},{2,6},{6,2},{3,7},{7,3},{8,12},{12,8},{9,1... | collective-permute-start | bytes 4718600 | tf_op jit(solution)/shard_map/ppermute | solution.py:553
  498.2 25.1 %collective-permute-start.55 = (bf16[288,768]{1,0:T(8,128)(2,1)S(1)}, bf16[288,768]{1,0:T(8,128)(2,1)S(1)}, u32[]{:S(2)}, u32[]{:S(2)}) collective-permute-start(bf16[288,768]{1,0:T(8,128)(2,1)S(1)} %get-tuple-element.377), channel_id=1, source_target_pairs={{0,1},{1,0},{2,3},{3,2},{4,5},{5,4},{6,7},{7,6},{8,9},{9,8},{10,11... | collective-permute-start | bytes 1327112 | tf_op jit(solution)/shard_map/ppermute | solution.py:557
  505.8 21.5 %collective-permute-start.58 = (bf16[1,768,256]{2,1,0:T(8,128)(2,1)S(1)}, bf16[1,768,256]{2,1,0:T(8,128)(2,1)S(1)}, u32[]{:S(2)}, u32[]{:S(2)}) collective-permute-start(bf16[1,768,256]{2,1,0:T(8,128)(2,1)S(1)} %copy-done.38), channel_id=1, source_target_pairs={{0,3},{1,2},{2,1},{3,0},{4,7},{5,6},{6,5},{7,4},{8,11},{9,10},{10,... | collective-permute-start | bytes 1179656 | tf_op jit(solution)/shard_map/ppermute | solution.py:557
  507.8 24.2 %collective-permute-start.56 = (bf16[288,768]{1,0:T(8,128)(2,1)S(1)}, bf16[288,768]{1,0:T(8,128)(2,1)S(1)}, u32[]{:S(2)}, u32[]{:S(2)}) collective-permute-start(bf16[288,768]{1,0:T(8,128)(2,1)S(1)} %get-tuple-element.378), channel_id=1, source_target_pairs={{0,1},{1,0},{2,3},{3,2},{4,5},{5,4},{6,7},{7,6},{8,9},{9,8},{10,11... | collective-permute-start | bytes 1327112 | tf_op jit(solution)/shard_map/ppermute | solution.py:557
  507.8 33.1 %collective-permute-start.61 = (bf16[3,768,256]{2,1,0:T(8,128)(2,1)S(1)}, bf16[3,768,256]{2,1,0:T(8,128)(2,1)S(1)}, u32[]{:S(2)}, u32[]{:S(2)}) collective-permute-start(bf16[3,768,256]{2,1,0:T(8,128)(2,1)S(1)} %copy-done.47), channel_id=1, source_target_pairs={{0,16},{16,0},{1,17},{17,1},{2,18},{18,2},{3,19},{19,3},{4,20},{20... | collective-permute-start | bytes 3538952 | tf_op jit(solution)/shard_map/ppermute | solution.py:553
  532.0 28.4 %collective-permute-start.62 = (bf16[3,768,256]{2,1,0:T(8,128)(2,1)S(1)}, bf16[3,768,256]{2,1,0:T(8,128)(2,1)S(1)}, u32[]{:S(2)}, u32[]{:S(2)}) collective-permute-start(bf16[3,768,256]{2,1,0:T(8,128)(2,1)S(1)} %copy-done.22), channel_id=1, source_target_pairs={{0,1},{1,0},{2,3},{3,2},{4,5},{5,4},{6,7},{7,6},{8,9},{9,8},{10,11... | collective-permute-start | bytes 3538952 | tf_op jit(solution)/shard_map/ppermute | solution.py:557
  534.1 34.0 %collective-permute-start.60 = (bf16[256,1536]{1,0:T(8,128)(2,1)S(1)}, bf16[256,1536]{1,0:T(8,128)(2,1)S(1)}, u32[]{:S(2)}, u32[]{:S(2)}) collective-permute-start(bf16[256,1536]{1,0:T(8,128)(2,1)S(1)} %fusion.10), channel_id=1, source_target_pairs={{0,8},{8,0},{1,9},{9,1},{2,10},{10,2},{3,11},{11,3},{4,12},{12,4},... | collective-permute-start | bytes 2359304 | tf_op jit(solution)/shard_map/ppermute | solution.py:553
  535.3 32.8 %collective-permute-start.59 = (bf16[288,768]{1,0:T(8,128)(2,1)S(1)}, bf16[288,768]{1,0:T(8,128)(2,1)S(1)}, u32[]{:S(2)}, u32[]{:S(2)}) collective-permute-start(bf16[288,768]{1,0:T(8,128)(2,1)S(1)} %add_convert_fusion.12), channel_id=1, source_target_pairs={{0,3},{1,2},{2,1},{3,0},{4,7},{5,6},{6,5},{7,4},{8,11},{9,10},{10,... | collective-permute-start | bytes 1327112 | tf_op jit(solution)/shard_map/ppermute | solution.py:557
  569.9 26.0 %collective-permute-start.68 = (bf16[3,192,256]{2,1,0:T(8,128)(2,1)}, bf16[3,192,256]{2,1,0:T(8,128)(2,1)}, u32[]{:S(2)}, u32[]{:S(2)}) collective-permute-start(bf16[3,192,256]{2,1,0:T(8,128)(2,1)} %get-tuple-element.414), channel_id=1, source_target_pairs={{0,12},{4,8},{8,4},{12,0},{1,13},{5,9},{9,5},{13,1},{2,14},{6,10},... | collective-permute-start | bytes 884744 | tf_op jit(solution)/shard_map/ppermute | solution.py:586
  570.0 26.0 %collective-permute-start.67 = (bf16[3,192,256]{2,1,0:T(8,128)(2,1)}, bf16[3,192,256]{2,1,0:T(8,128)(2,1)}, u32[]{:S(2)}, u32[]{:S(2)}) collective-permute-start(bf16[3,192,256]{2,1,0:T(8,128)(2,1)} %get-tuple-element.415), channel_id=1, source_target_pairs={{0,8},{8,0},{1,9},{9,1},{2,10},{10,2},{3,11},{11,3},{4,12},{12,4},... | collective-permute-start | bytes 884744 | tf_op jit(solution)/shard_map/ppermute | solution.py:553
  571.2 24.7 %collective-permute-start.66 = (bf16[3,192,256]{2,1,0:T(8,128)(2,1)}, bf16[3,192,256]{2,1,0:T(8,128)(2,1)}, u32[]{:S(2)}, u32[]{:S(2)}) collective-permute-start(bf16[3,192,256]{2,1,0:T(8,128)(2,1)} %get-tuple-element.416), channel_id=1, source_target_pairs={{0,4},{4,0},{1,5},{5,1},{2,6},{6,2},{3,7},{7,3},{8,12},{12,8},{9,1... | collective-permute-start | bytes 884744 | tf_op jit(solution)/shard_map/ppermute | solution.py:553
  (105 other events, 1373.1 us)
